TPU v7x, 32 devices: a whole 2x2x4 slice. The times are simulated.
32 devices in a mesh: pts: 16 (over z, y, x), rep: 2 (over core).
Axes of the slice: x: 2, y: 2, z: 4, core: 2. Of those that a mesh axis runs over, the one named last changes fastest.
Arguments:
- src_points: bfloat16 [49152, 256], P('pts'), may hold values from -7 to 7
- tgt_points: bfloat16 [49152, 256], P('pts'), may hold values from -7 to 7
- pair_source: int32 [512], P(('pts', 'rep')), may hold values from -1 to 383, as said below
- pair_target: int32 [512], P(('pts', 'rep')), may hold values from -1 to 383, as said below
- pair_count: int32 [32], P(('pts', 'rep')), may hold values from 12 to 16, as said below
Outputs:
- source_dual: float32 [49152], P('pts')
- target_dual: float32 [49152], P('pts')
- target_grad: float32 [49152, 256], P('pts')
Inputs may be any that keep to these rules, and one draw needn't show every extreme that they name: `pair_source`: for the device at index d of pts+rep (pts index p = d // 2, rep index r = d % 2), the first pair_count[d] of its 16 slots name source blocks p * 24 to (p + 1) * 24 - 1; its other slots hold -1. `pair_target`: A listed target block t has owner t // 24; one device's listed slots name different owners, and only blocks whose index t % 24 lies in r * 12 to (r + 1) * 12 - 1; unlisted slots hold -1. No pair of blocks is listed twice; every source block and every target block is listed somewhere; some owner is named by every device. `pair_count`: some device lists 16 pairs.
All inputs are finite; a program needn't handle non-finite values.
Results may differ from a plain program's by a relative error of at most 0.0016.
Values may be sent and summed in bfloat16 or wider, within the bound.
A program may use at most 192 MiB of HBM per device.

v0:
```python
import jax
import jax.numpy as jnp
from jax import lax
from jax.sharding import PartitionSpec as P

BLOCK = 128
ITERS = 3


EPSILON = 0.05
NEG_BIG = -1e30


def joined(part, axis, combine):
    gathered = jax.tree.map(lambda a: lax.all_gather(a, axis), part)

    def take(source):
        return jax.tree.map(lambda a: lax.dynamic_index_in_dim(a, source, 0, False), gathered)

    return lax.fori_loop(
        1, lax.axis_size(axis), lambda source, state: combine(state, take(source)), take(0)
    )


def squares(blocks_in):
    return jnp.sum(jnp.square(blocks_in.astype(jnp.float32)), axis=-1)


def pair_costs(source_rows, target_rows, source_sq, target_sq):
    inner_dot = jnp.einsum(
        "gid,gjd->gij", source_rows, target_rows, preferred_element_type=jnp.float32
    )
    return (source_sq[:, :, None] + target_sq[:, None, :] - 2.0 * inner_dot) / source_rows.shape[2]


def pair_sweep(arranged, pair_total, visit, initial):
    source_slots, source_sq_slots, target_slots, target_sq_slots = arranged

    def advance(group_no, carry):
        first_row = group_no * 8
        in_use = first_row + jnp.arange(8) < pair_total
        source_rows = lax.dynamic_slice_in_dim(source_slots, first_row, 8)
        target_rows = lax.dynamic_slice_in_dim(target_slots, first_row, 8)
        source_sq = lax.dynamic_slice_in_dim(source_sq_slots, first_row, 8)
        target_sq = lax.dynamic_slice_in_dim(target_sq_slots, first_row, 8)
        cost_grid = pair_costs(source_rows, target_rows, source_sq, target_sq)
        return visit(carry, cost_grid, source_rows, in_use, first_row)

    return lax.fori_loop(0, (pair_total + 7) // 8, advance, initial)


def store_stats(carry, peaks, masses, in_use, first_row):
    peaks = jnp.where(in_use[:, None], peaks, NEG_BIG)
    masses = jnp.where(in_use[:, None], masses, 0.0)
    return (
        lax.dynamic_update_slice_in_dim(carry[0], peaks, first_row, 0),
        lax.dynamic_update_slice_in_dim(carry[1], masses, first_row, 0),
    )


def row_visit(target_dual_slots):

    def visit(carry, cost_grid, source_rows, in_use, first_row):
        duals_here = lax.dynamic_slice_in_dim(target_dual_slots, first_row, 8)
        scores = (duals_here[:, None, :] - cost_grid) / EPSILON
        peaks = jnp.max(scores, axis=2)
        masses = jnp.sum(jnp.exp(scores - peaks[:, :, None]), axis=2)
        return store_stats(carry, peaks, masses, in_use, first_row)

    return visit


def column_visit(source_dual_slots):

    def visit(carry, cost_grid, source_rows, in_use, first_row):
        duals_here = lax.dynamic_slice_in_dim(source_dual_slots, first_row, 8)
        scores = (duals_here[:, :, None] - cost_grid) / EPSILON
        peaks = jnp.max(scores, axis=1)
        masses = jnp.sum(jnp.exp(scores - peaks[:, None, :]), axis=1)
        return store_stats(carry, peaks, masses, in_use, first_row)

    return visit


def gradient_visit(source_dual_slots, target_dual_slots):

    def visit(carry, cost_grid, source_rows, in_use, first_row):
        partials, masses = carry
        source_here = lax.dynamic_slice_in_dim(source_dual_slots, first_row, 8)
        target_here = lax.dynamic_slice_in_dim(target_dual_slots, first_row, 8)
        plan = jnp.exp((source_here[:, :, None] + target_here[:, None, :] - cost_grid) / EPSILON)
        plan = jnp.where(in_use[:, None, None], plan, 0.0)
        partial_value = jnp.einsum(
            "gij,gid->gjd",
            plan.astype(jnp.bfloat16),
            source_rows,
            preferred_element_type=jnp.float32,
        )
        partials = lax.dynamic_update_slice_in_dim(partials, partial_value, first_row, 0)
        masses = lax.dynamic_update_slice_in_dim(masses, jnp.sum(plan, axis=1), first_row, 0)
        return (partials, masses)

    return visit


def fresh_stats(length, block_len):
    return (
        jnp.full((length, block_len), NEG_BIG, jnp.float32),
        jnp.zeros((length, block_len), jnp.float32),
    )


def combine_by(peaks, masses, block_key, key_count):
    member = (block_key[:, None] == jnp.arange(key_count)[None, :])[:, :, None]
    maxima = jnp.max(jnp.where(member, peaks[:, None, :], NEG_BIG), axis=0)
    shifts = jnp.where(member, peaks[:, None, :] - maxima[None, :, :], NEG_BIG)
    totals = jnp.sum(jnp.where(member, masses[:, None, :] * jnp.exp(shifts), 0.0), axis=0)
    return (maxima, totals)


def merge_logsum(former, latter):
    maxima = jnp.maximum(former[0], latter[0])
    return (
        maxima,
        former[1] * jnp.exp(former[0] - maxima) + latter[1] * jnp.exp(latter[0] - maxima),
    )


def settle_sources(peaks, masses, block_key, key_count):
    maxima, totals = combine_by(peaks, masses, block_key, key_count)
    maxima, totals = joined((maxima, totals), "rep", merge_logsum)
    return -EPSILON * (maxima + jnp.log(totals))


def settle_targets(maxima, totals, half_blocks):
    lower_row = lax.axis_index("rep") * half_blocks
    maxima_half = lax.dynamic_slice_in_dim(maxima, lower_row, half_blocks, 0)
    totals_half = lax.dynamic_slice_in_dim(totals, lower_row, half_blocks, 0)
    dual_half = -EPSILON * (maxima_half + jnp.log(totals_half))
    return lax.all_gather(dual_half, "rep", axis=0, tiled=True)


def owner_pairs(asked_ids):
    ranking = jnp.argsort(jnp.where(asked_ids >= 0, 0, 1), stable=True)
    pair_total = jnp.sum((asked_ids >= 0).astype(jnp.int32))
    return (ranking, jnp.maximum(asked_ids[ranking], 0), pair_total)


def collect_by(partials, masses, block_key, key_count):
    member = (block_key[:, None] == jnp.arange(key_count)[None, :]).astype(jnp.float32)
    numerator = jnp.einsum("sb,sjd->bjd", member, partials, precision=lax.Precision.HIGHEST)
    column_mass = jnp.einsum("sb,sj->bj", member, masses, precision=lax.Precision.HIGHEST)
    return (numerator, column_mass)


def on_device(src_points, tgt_points, pair_source, pair_target, pair_count):
    peer_count = lax.axis_size("pts")
    point_rows, feat_width = src_points.shape
    block_len = BLOCK
    blocks = point_rows // block_len
    half_blocks = blocks // lax.axis_size("rep")
    own_sources = src_points.reshape(blocks, block_len, feat_width)
    own_targets = tgt_points.reshape(blocks, block_len, feat_width)
    source_sq = squares(own_sources)
    target_sq = squares(own_targets)
    pair_total = pair_count[0]
    slot_total = pair_source.shape[0]
    usable = jnp.arange(slot_total) < pair_total
    source_local = jnp.where(usable, pair_source % blocks, 0)
    owner_ids = jnp.where(usable, pair_target // blocks, 0)
    target_local = jnp.where(usable, pair_target % blocks, 0)
    matched = (owner_ids[:, None] == jnp.arange(peer_count)[None, :]) & usable[:, None]
    wanted = jnp.max(jnp.where(matched, target_local[:, None], -1), axis=0)
    source_of_owner = jnp.max(jnp.where(matched, source_local[:, None], -1), axis=0)
    served = source_of_owner >= 0
    source_index = jnp.maximum(source_of_owner, 0)
    outgoing = jnp.where(
        served[:, None, None], own_sources[source_index], jnp.zeros((), src_points.dtype)
    )
    asked_ids = lax.all_to_all(wanted, "pts", split_axis=0, concat_axis=0, tiled=True)
    replies = jnp.where(
        (asked_ids >= 0)[:, None, None],
        own_targets[jnp.maximum(asked_ids, 0)],
        jnp.zeros((), tgt_points.dtype),
    )
    fetched = lax.all_to_all(replies, "pts", split_axis=0, concat_axis=0, tiled=True)
    fetched_sq = squares(fetched)
    sweep_slots = (
        own_sources[source_local],
        source_sq[source_local],
        fetched[owner_ids],
        fetched_sq[owner_ids],
    )
    target_slices = jnp.zeros((peer_count, block_len), jnp.float32)
    owner_drop = jnp.where(usable, owner_ids, peer_count)
    for round_no in range(ITERS):
        peaks, masses = pair_sweep(
            sweep_slots,
            pair_total,
            row_visit(target_slices[owner_ids]),
            fresh_stats(slot_total, block_len),
        )
        source_dual = settle_sources(peaks, masses, jnp.where(usable, source_local, -1), blocks)
        peaks, masses = pair_sweep(
            sweep_slots,
            pair_total,
            column_visit(source_dual[source_local]),
            fresh_stats(slot_total, block_len),
        )
        out_peaks = (
            jnp.full((peer_count, block_len), NEG_BIG, jnp.float32)
            .at[owner_drop]
            .set(peaks, mode="drop")
        )
        out_masses = (
            jnp.zeros((peer_count, block_len), jnp.float32).at[owner_drop].set(masses, mode="drop")
        )
        in_peaks, in_masses = (
            lax.all_to_all(out_peaks, "pts", split_axis=0, concat_axis=0, tiled=True),
            lax.all_to_all(out_masses, "pts", split_axis=0, concat_axis=0, tiled=True),
        )
        maxima, totals = combine_by(in_peaks, in_masses, asked_ids, blocks)
        target_dual = settle_targets(maxima, totals, half_blocks)
        if round_no + 1 < ITERS:
            returned = jnp.where(
                (asked_ids >= 0)[:, None], target_dual[jnp.maximum(asked_ids, 0)], 0.0
            )
            target_slices = lax.all_to_all(returned, "pts", split_axis=0, concat_axis=0, tiled=True)
    received = lax.all_to_all(outgoing, "pts", split_axis=0, concat_axis=0, tiled=True)
    sent_duals = jnp.where(served[:, None], source_dual[source_index], 0.0)
    received_duals = lax.all_to_all(sent_duals, "pts", split_axis=0, concat_axis=0, tiled=True)
    ranking, target_pick, received_total = owner_pairs(asked_ids)
    received_sq = squares(received)
    owner_slots = (
        received[ranking],
        received_sq[ranking],
        own_targets[target_pick],
        target_sq[target_pick],
    )
    start_sums = (
        jnp.zeros((peer_count, block_len, feat_width), jnp.float32),
        jnp.zeros((peer_count, block_len), jnp.float32),
    )
    partials, masses = pair_sweep(
        owner_slots,
        received_total,
        gradient_visit(received_duals[ranking], target_dual[target_pick]),
        start_sums,
    )
    gradient_key = jnp.where(jnp.arange(peer_count) < received_total, target_pick, -1)
    numerator, column_mass = collect_by(partials, masses, gradient_key, blocks)
    lower_row = lax.axis_index("rep") * half_blocks
    target_half = lax.dynamic_slice_in_dim(own_targets, lower_row, half_blocks, 0).astype(
        jnp.float32
    )
    mass_half = lax.dynamic_slice_in_dim(column_mass, lower_row, half_blocks, 0)
    numerator_half = lax.dynamic_slice_in_dim(numerator, lower_row, half_blocks, 0)
    gradient_half = target_half * mass_half[:, :, None] - numerator_half
    gradient = lax.all_gather(gradient_half, "rep", axis=0, tiled=True)
    return (
        source_dual.reshape(-1),
        target_dual.reshape(-1),
        gradient.reshape(blocks * block_len, feat_width),
    )


def solution(mesh):
    return jax.shard_map(
        on_device,
        mesh=mesh,
        in_specs=(
            P("pts", None),
            P("pts", None),
            P(("pts", "rep")),
            P(("pts", "rep")),
            P(("pts", "rep")),
        ),
        out_specs=(P("pts"), P("pts"), P("pts", None)),
        check_vma=False,
    )
```

profile of v0, /device:TPU:0, one launch (start us, length us, event | category | flops | bytes accessed | tf_op | source)
XLA Modules:
  0.0 272.2 jit_solution(3842884084834779802)
XLA Ops:
  9.3 15.4 %all_to_all.103 = s32[16,1,1]{2,1,0:T(1,128)S(1)} all-to-all(s32[16,1,1]{2,1,0:T(1,128)S(1)} %copy.53), channel_id=1, replica_groups=mesh['pts'=16,'rep'=2] {'pts'}, dimensions={0} | all-to-all | bytes 128 | tf_op jit(solution)/shard_map/all_to_all | solution.py:180
  25.4 2.0 gather_fusion.2
  28.9 3.7 %all-to-all-start.1 = ((bf16[16,128,256]{2,1,0:T(8,128)(2,1)}), bf16[16,128,256]{2,1,0:T(8,128)(2,1)S(1)}, u32[]{:S(2)}, u32[]{:S(2)}) async-start(bf16[16,128,256]{2,1,0:T(8,128)(2,1)} %broadcast_select_fusion.1), calls=%async_computation.1 | async-start | bytes 2097152 | tf_op jit(solution)/shard_map/all_to_all | solution.py:186
  33.7 1.6 gather_fusion.4
  36.1 19.8 %all-to-all-done.1 = bf16[16,128,256]{2,1,0:T(8,128)(2,1)S(1)} async-done(((bf16[16,128,256]{2,1,0:T(8,128)(2,1)}), bf16[16,128,256]{2,1,0:T(8,128)(2,1)S(1)}, u32[]{:S(2)}, u32[]{:S(2)}) %all-to-all-start.1) | async-done | bytes 1048608 | tf_op jit(solution)/shard_map/all_to_all | solution.py:186
  58.4 4.9 %while.31 = (s32[]{:T(128)}, f32[16,128]{1,0:T(8,128)S(1)}, f32[16,128]{1,0:T(8,128)S(1)}, s32[]{:T(128)}, s32[]{:T(128)}, /*index=5*/f32[16,128]{1,0:T(8,128)S(...) while((s32[]{:T(128)}, f32[16,128]{1,0:T(8,128)S(1)}, ...), condition=%wide.region_6.7_spmd, body=%wide.region_3.6_spmd.sunk | while | flops 68288536 | bytes 2164439 | solution.py:49
  63.3 1.8 all-gather
  65.3 1.8 all-gather.1
  67.7 4.9 %while.32 = (s32[]{:T(128)}, f32[16,128]{1,0:T(8,128)S(1)}, f32[16,128]{1,0:T(8,128)S(1)}, s32[]{:T(128)}, s32[]{:T(128)}, /*index=5*/f32[16,128]{1,0:T(8,128)S(...) while((s32[]{:T(128)}, f32[16,128]{1,0:T(8,128)S(1)}, ...), condition=%wide.region_12.13_spmd, body=%wide.region_9.12_spmd.sunk | while | flops 68288536 | bytes 2164439 | solution.py:49
  73.8 5.8 %all-to-all-start.2 = ((f32[16,1,128]{2,1,0:T(1,128)}), f32[16,1,128]{2,1,0:T(1,128)S(1)}, u32[]{:S(2)}, u32[]{:S(2)}) async-start(f32[16,1,128]{2,1,0:T(1,128)} %bitcast.5), calls=%async_computation.2 | async-start | bytes 16384 | tf_op jit(solution)/shard_map/all_to_all | solution.py:219
  80.8 6.0 %all-to-all-done.2 = f32[16,1,128]{2,1,0:T(1,128)S(1)} async-done(((f32[16,1,128]{2,1,0:T(1,128)}), f32[16,1,128]{2,1,0:T(1,128)S(1)}, u32[]{:S(2)}, u32[]{:S(2)}) %all-to-all-start.2) | async-done | bytes 8224 | tf_op jit(solution)/shard_map/all_to_all | solution.py:219
  86.8 3.5 %all-to-all-start.3 = ((f32[16,1,128]{2,1,0:T(1,128)}), f32[16,1,128]{2,1,0:T(1,128)S(1)}, u32[]{:S(2)}, u32[]{:S(2)}) async-start(f32[16,1,128]{2,1,0:T(1,128)} %bitcast.8), calls=%async_computation.3 | async-start | bytes 16384 | tf_op jit(solution)/shard_map/all_to_all | solution.py:220
  90.4 7.0 %all-to-all-done.3 = f32[16,1,128]{2,1,0:T(1,128)S(1)} async-done(((f32[16,1,128]{2,1,0:T(1,128)}), f32[16,1,128]{2,1,0:T(1,128)S(1)}, u32[]{:S(2)}, u32[]{:S(2)}) %all-to-all-start.3) | async-done | bytes 8224 | tf_op jit(solution)/shard_map/all_to_all | solution.py:220
  97.6 1.8 all-gather.6
  100.7 3.5 %all-to-all-start.4 = ((f32[16,1,128]{2,1,0:T(1,128)}), f32[16,1,128]{2,1,0:T(1,128)S(1)}, u32[]{:S(2)}, u32[]{:S(2)}) async-start(f32[16,1,128]{2,1,0:T(1,128)} %bitcast.12), calls=%async_computation.4 | async-start | bytes 16384 | tf_op jit(solution)/shard_map/all_to_all | solution.py:228
  104.2 7.2 %all-to-all-done.4 = f32[16,1,128]{2,1,0:T(1,128)S(1)} async-done(((f32[16,1,128]{2,1,0:T(1,128)}), f32[16,1,128]{2,1,0:T(1,128)S(1)}, u32[]{:S(2)}, u32[]{:S(2)}) %all-to-all-start.4) | async-done | bytes 8224 | tf_op jit(solution)/shard_map/all_to_all | solution.py:228
  111.9 4.9 %while.33 = (s32[]{:T(128)}, f32[16,128]{1,0:T(8,128)S(1)}, f32[16,128]{1,0:T(8,128)S(1)}, s32[]{:T(128)}, s32[]{:T(128)}, /*index=5*/f32[16,128]{1,0:T(8,128)S(...) while((s32[]{:T(128)}, f32[16,128]{1,0:T(8,128)S(1)}, ...), condition=%wide.region_20.21_spmd, body=%wide.region_17.20_spmd.sunk | while | flops 68288536 | bytes 2164439 | solution.py:49
  116.9 1.8 all-gather.2
  118.9 1.8 all-gather.3
  121.3 4.9 %while.34 = (s32[]{:T(128)}, f32[16,128]{1,0:T(8,128)S(1)}, f32[16,128]{1,0:T(8,128)S(1)}, s32[]{:T(128)}, s32[]{:T(128)}, /*index=5*/f32[16,128]{1,0:T(8,128)S(...) while((s32[]{:T(128)}, f32[16,128]{1,0:T(8,128)S(1)}, ...), condition=%wide.region_26.27_spmd, body=%wide.region_23.26_spmd.sunk | while | flops 68288536 | bytes 2164439 | solution.py:49
  127.4 3.5 %all-to-all-start.5 = ((f32[16,1,128]{2,1,0:T(1,128)}), f32[16,1,128]{2,1,0:T(1,128)S(1)}, u32[]{:S(2)}, u32[]{:S(2)}) async-start(f32[16,1,128]{2,1,0:T(1,128)} %bitcast.15), calls=%async_computation.5 | async-start | bytes 16384 | tf_op jit(solution)/shard_map/all_to_all | solution.py:219
  133.7 4.4 %all-to-all-done.5 = f32[16,1,128]{2,1,0:T(1,128)S(1)} async-done(((f32[16,1,128]{2,1,0:T(1,128)}), f32[16,1,128]{2,1,0:T(1,128)S(1)}, u32[]{:S(2)}, u32[]{:S(2)}) %all-to-all-start.5) | async-done | bytes 8224 | tf_op jit(solution)/shard_map/all_to_all | solution.py:219
  138.1 3.5 %all-to-all-start.6 = ((f32[16,1,128]{2,1,0:T(1,128)}), f32[16,1,128]{2,1,0:T(1,128)S(1)}, u32[]{:S(2)}, u32[]{:S(2)}) async-start(f32[16,1,128]{2,1,0:T(1,128)} %bitcast.18), calls=%async_computation.6 | async-start | bytes 16384 | tf_op jit(solution)/shard_map/all_to_all | solution.py:220
  141.6 2.5 broadcast_select_fusion
  144.0 4.7 %all-to-all-done.6 = f32[16,1,128]{2,1,0:T(1,128)S(1)} async-done(((f32[16,1,128]{2,1,0:T(1,128)}), f32[16,1,128]{2,1,0:T(1,128)S(1)}, u32[]{:S(2)}, u32[]{:S(2)}) %all-to-all-start.6) | async-done | bytes 8224 | tf_op jit(solution)/shard_map/all_to_all | solution.py:220
  148.7 3.7 %all-to-all-start.11 = ((bf16[16,128,256]{2,1,0:T(8,128)(2,1)}), bf16[16,128,256]{2,1,0:T(8,128)(2,1)S(1)}, u32[]{:S(2)}, u32[]{:S(2)}) async-start(bf16[16,128,256]{2,1,0:T(8,128)(2,1)} %broadcast_select_fusion), calls=%async_computation.11 | async-start | bytes 2097152 | tf_op jit(solution)/shard_map/all_to_all | solution.py:229
  157.7 1.6 gather_fusion.21
  160.2 1.8 all-gather.7
  163.2 11.8 %all-to-all-done.11 = bf16[16,128,256]{2,1,0:T(8,128)(2,1)S(1)} async-done(((bf16[16,128,256]{2,1,0:T(8,128)(2,1)}), bf16[16,128,256]{2,1,0:T(8,128)(2,1)S(1)}, u32[]{:S(2)}, u32[]{:S(2)}) %all-to-all-start.11) | async-done | bytes 1048608 | tf_op jit(solution)/shard_map/all_to_all | solution.py:229
  175.1 6.0 %all-to-all-start.7 = ((f32[16,1,128]{2,1,0:T(1,128)}), f32[16,1,128]{2,1,0:T(1,128)S(1)}, u32[]{:S(2)}, u32[]{:S(2)}) async-start(f32[16,1,128]{2,1,0:T(1,128)} %bitcast.22), calls=%async_computation.7 | async-start | bytes 16384 | tf_op jit(solution)/shard_map/all_to_all | solution.py:228
  182.6 5.7 %all-to-all-done.7 = f32[16,1,128]{2,1,0:T(1,128)S(1)} async-done(((f32[16,1,128]{2,1,0:T(1,128)}), f32[16,1,128]{2,1,0:T(1,128)S(1)}, u32[]{:S(2)}, u32[]{:S(2)}) %all-to-all-start.7) | async-done | bytes 8224 | tf_op jit(solution)/shard_map/all_to_all | solution.py:228
  188.8 4.9 %while.106 = (s32[]{:T(128)}, f32[16,128]{1,0:T(8,128)S(1)}, f32[16,128]{1,0:T(8,128)S(1)}, s32[]{:T(128)}, s32[]{:T(128)}, /*index=5*/f32[16,128]{1,0:T(8,128)S...) while((s32[]{:T(128)}, f32[16,128]{1,0:T(8,128)S(1)}, ...), condition=%wide.region_34.35_spmd, body=%wide.region_31.34_spmd.sunk | while | flops 68288536 | bytes 2164439 | solution.py:49
  193.8 1.8 all-gather.4
  195.8 1.8 all-gather.5
  198.8 4.9 %while.107 = (s32[]{:T(128)}, f32[16,128]{1,0:T(8,128)S(1)}, f32[16,128]{1,0:T(8,128)S(1)}, s32[]{:T(128)}, s32[]{:T(128)}, /*index=5*/f32[16,128]{1,0:T(8,128)S...) while((s32[]{:T(128)}, f32[16,128]{1,0:T(8,128)S(1)}, ...), condition=%wide.region_40.41_spmd, body=%wide.region_37.40_spmd.sunk | while | flops 68288536 | bytes 2164439 | solution.py:49
  204.9 3.5 %all-to-all-start.8 = ((f32[16,1,128]{2,1,0:T(1,128)}), f32[16,1,128]{2,1,0:T(1,128)S(1)}, u32[]{:S(2)}, u32[]{:S(2)}) async-start(f32[16,1,128]{2,1,0:T(1,128)} %bitcast.29), calls=%async_computation.8 | async-start | bytes 16384 | tf_op jit(solution)/shard_map/all_to_all | solution.py:219
  210.2 5.3 %all-to-all-done.8 = f32[16,1,128]{2,1,0:T(1,128)S(1)} async-done(((f32[16,1,128]{2,1,0:T(1,128)}), f32[16,1,128]{2,1,0:T(1,128)S(1)}, u32[]{:S(2)}, u32[]{:S(2)}) %all-to-all-start.8) | async-done | bytes 8224 | tf_op jit(solution)/shard_map/all_to_all | solution.py:219
  215.5 3.7 %all-to-all-start.9 = ((f32[16,1,128]{2,1,0:T(1,128)}), f32[16,1,128]{2,1,0:T(1,128)S(1)}, u32[]{:S(2)}, u32[]{:S(2)}) async-start(f32[16,1,128]{2,1,0:T(1,128)} %bitcast.32), calls=%async_computation.9 | async-start | bytes 16384 | tf_op jit(solution)/shard_map/all_to_all | solution.py:220
  219.3 6.9 %all-to-all-done.9 = f32[16,1,128]{2,1,0:T(1,128)S(1)} async-done(((f32[16,1,128]{2,1,0:T(1,128)}), f32[16,1,128]{2,1,0:T(1,128)S(1)}, u32[]{:S(2)}, u32[]{:S(2)}) %all-to-all-start.9) | async-done | bytes 8224 | tf_op jit(solution)/shard_map/all_to_all | solution.py:220
  226.2 3.5 %all-to-all-start.10 = ((f32[16,1,128]{2,1,0:T(1,128)}), f32[16,1,128]{2,1,0:T(1,128)S(1)}, u32[]{:S(2)}, u32[]{:S(2)}) async-start(f32[16,1,128]{2,1,0:T(1,128)} %bitcast.36), calls=%async_computation.10 | async-start | bytes 16384 | tf_op jit(solution)/shard_map/all_to_all | solution.py:231
  229.9 1.8 all-gather.8
  231.7 5.1 %all-to-all-done.10 = f32[16,1,128]{2,1,0:T(1,128)S(1)} async-done(((f32[16,1,128]{2,1,0:T(1,128)}), f32[16,1,128]{2,1,0:T(1,128)S(1)}, u32[]{:S(2)}, u32[]{:S(2)}) %all-to-all-start.10) | async-done | bytes 8224 | tf_op jit(solution)/shard_map/all_to_all | solution.py:231
  239.5 6.0 %while.108 = (s32[]{:T(128)}, f32[16,128,256]{2,0,1:T(8,128)}, f32[16,128]{1,0:T(8,128)S(1)}, s32[]{:T(128)}, s32[]{:T(128)}, /*index=5*/f32[16,128]{1,0:T(8,128...) while((s32[]{:T(128)}, f32[16,128,256]{2,0,1:T(8,128)}, ...), condition=%wide.region_52.53_spmd, body=%wide.region_50.52_spmd.sunk | while | flops 135527456 | bytes 5306087 | solution.py:49
  245.6 3.1 %fusion.77 = f32[24,128,256]{2,0,1:T(8,128)S(1)} fusion(f32[16,128,256]{2,0,1:T(8,128)} %get-tuple-element.455, s32[16]{0:T(128)S(1)} %get-tuple-element.719), kind=kOutput, calls=%fused_computation.206 | convolution fusion | flops 150995328 | bytes 5242944 | tf_op jit(solution)/shard_map/sb,sjd->bjd/dot_general | solution.py:151
  249.1 1.8 dynamic-slice_subtract_fusion
  250.9 2.1 copy.65
  254.2 7.4 %all-gather.11.cloned.1.call-done = f32[24,128,256]{2,1,0:T(8,128)} async-done(((f32[12,128,256]{2,1,0:T(8,128)}), f32[24,128,256]{2,1,0:T(8,128)}) %all-gather.11.cloned.1.call-update) | async-done | bytes 3145744 | tf_op jit(solution)/shard_map/all_gather | solution.py:259
  261.6 3.8 %copy.169 = f32[3072,256]{1,0:T(8,128)} copy(f32[3072,256]{1,0:T(8,128)} %bitcast.96) | data formatting | bytes 6291456
  (192 shorter events, 70.7 us)
Async XLA Ops:
  27.8 4.8 %copy-start.1 = (bf16[3072,256]{1,0:T(8,128)(2,1)S(1)}, bf16[3072,256]{1,0:T(8,128)(2,1)}, u32[]{:S(2)}) copy-start(bf16[3072,256]{1,0:T(8,128)(2,1)} %param.19) | copy-start | bytes 4718596
  28.9 26.9 %all-to-all-start.1 = ((bf16[16,128,256]{2,1,0:T(8,128)(2,1)}), bf16[16,128,256]{2,1,0:T(8,128)(2,1)S(1)}, u32[]{:S(2)}, u32[]{:S(2)}) async-start(bf16[16,128,256]{2,1,0:T(8,128)(2,1)} %broadcast_select_fusion.1), calls=%async_computation.1 | async-start | bytes 2097152 | tf_op jit(solution)/shard_map/all_to_all | solution.py:186
  73.8 13.0 %all-to-all-start.2 = ((f32[16,1,128]{2,1,0:T(1,128)}), f32[16,1,128]{2,1,0:T(1,128)S(1)}, u32[]{:S(2)}, u32[]{:S(2)}) async-start(f32[16,1,128]{2,1,0:T(1,128)} %bitcast.5), calls=%async_computation.2 | async-start | bytes 16384 | tf_op jit(solution)/shard_map/all_to_all | solution.py:219
  86.8 10.6 %all-to-all-start.3 = ((f32[16,1,128]{2,1,0:T(1,128)}), f32[16,1,128]{2,1,0:T(1,128)S(1)}, u32[]{:S(2)}, u32[]{:S(2)}) async-start(f32[16,1,128]{2,1,0:T(1,128)} %bitcast.8), calls=%async_computation.3 | async-start | bytes 16384 | tf_op jit(solution)/shard_map/all_to_all | solution.py:220
  100.7 10.6 %all-to-all-start.4 = ((f32[16,1,128]{2,1,0:T(1,128)}), f32[16,1,128]{2,1,0:T(1,128)S(1)}, u32[]{:S(2)}, u32[]{:S(2)}) async-start(f32[16,1,128]{2,1,0:T(1,128)} %bitcast.12), calls=%async_computation.4 | async-start | bytes 16384 | tf_op jit(solution)/shard_map/all_to_all | solution.py:228
  127.4 10.6 %all-to-all-start.5 = ((f32[16,1,128]{2,1,0:T(1,128)}), f32[16,1,128]{2,1,0:T(1,128)S(1)}, u32[]{:S(2)}, u32[]{:S(2)}) async-start(f32[16,1,128]{2,1,0:T(1,128)} %bitcast.15), calls=%async_computation.5 | async-start | bytes 16384 | tf_op jit(solution)/shard_map/all_to_all | solution.py:219
  138.1 10.6 %all-to-all-start.6 = ((f32[16,1,128]{2,1,0:T(1,128)}), f32[16,1,128]{2,1,0:T(1,128)S(1)}, u32[]{:S(2)}, u32[]{:S(2)}) async-start(f32[16,1,128]{2,1,0:T(1,128)} %bitcast.18), calls=%async_computation.6 | async-start | bytes 16384 | tf_op jit(solution)/shard_map/all_to_all | solution.py:220
  141.5 10.8 %copy-start = (bf16[3072,256]{1,0:T(8,128)(2,1)S(1)}, bf16[3072,256]{1,0:T(8,128)(2,1)}, u32[]{:S(2)}) copy-start(bf16[3072,256]{1,0:T(8,128)(2,1)} %param.20) | copy-start | bytes 4718596
  148.7 26.3 %all-to-all-start.11 = ((bf16[16,128,256]{2,1,0:T(8,128)(2,1)}), bf16[16,128,256]{2,1,0:T(8,128)(2,1)S(1)}, u32[]{:S(2)}, u32[]{:S(2)}) async-start(bf16[16,128,256]{2,1,0:T(8,128)(2,1)} %broadcast_select_fusion), calls=%async_computation.11 | async-start | bytes 2097152 | tf_op jit(solution)/shard_map/all_to_all | solution.py:229
  175.1 13.2 %all-to-all-start.7 = ((f32[16,1,128]{2,1,0:T(1,128)}), f32[16,1,128]{2,1,0:T(1,128)S(1)}, u32[]{:S(2)}, u32[]{:S(2)}) async-start(f32[16,1,128]{2,1,0:T(1,128)} %bitcast.22), calls=%async_computation.7 | async-start | bytes 16384 | tf_op jit(solution)/shard_map/all_to_all | solution.py:228
  203.7 35.8 %copy-start.2 = (bf16[16,128,256]{2,1,0:T(8,128)(2,1)S(1)}, bf16[16,128,256]{2,1,0:T(8,128)(2,1)}, u32[]{:S(2)}) copy-start(bf16[16,128,256]{2,1,0:T(8,128)(2,1)} %gather_fusion.21) | copy-start | bytes 3145732
  204.9 10.6 %all-to-all-start.8 = ((f32[16,1,128]{2,1,0:T(1,128)}), f32[16,1,128]{2,1,0:T(1,128)S(1)}, u32[]{:S(2)}, u32[]{:S(2)}) async-start(f32[16,1,128]{2,1,0:T(1,128)} %bitcast.29), calls=%async_computation.8 | async-start | bytes 16384 | tf_op jit(solution)/shard_map/all_to_all | solution.py:219
  215.5 10.6 %all-to-all-start.9 = ((f32[16,1,128]{2,1,0:T(1,128)}), f32[16,1,128]{2,1,0:T(1,128)S(1)}, u32[]{:S(2)}, u32[]{:S(2)}) async-start(f32[16,1,128]{2,1,0:T(1,128)} %bitcast.32), calls=%async_computation.9 | async-start | bytes 16384 | tf_op jit(solution)/shard_map/all_to_all | solution.py:220
  226.2 10.6 %all-to-all-start.10 = ((f32[16,1,128]{2,1,0:T(1,128)}), f32[16,1,128]{2,1,0:T(1,128)S(1)}, u32[]{:S(2)}, u32[]{:S(2)}) async-start(f32[16,1,128]{2,1,0:T(1,128)} %bitcast.36), calls=%async_computation.10 | async-start | bytes 16384 | tf_op jit(solution)/shard_map/all_to_all | solution.py:231
  229.7 32.0 %all-gather.11.cloned.1.call-start = ((), (), s32[]{:S(2)}) async-start(), calls=%async_computation.12 | async-start | bytes 4718592 | tf_op jit(solution)/shard_map/all_gather | solution.py:259
Sparse Core Ops, SparseCore 0:
  253.1 8.4 all-gather.10
where the time goes:
time: 274 us; the launch traced here: 272 us
  waiting for transfers between devices  91.3 us (33%)
  starting transfers between devices  43.6 us (16%)
  local copies, waits for them, and re-layouts  37.8 us (14%)
  blocking collectives  31.8 us (12%)
  other arithmetic  27.5 us (10%)
  matrix products  23.9 us (9%)
  between operations  15.9 us (6%)
    all_to_all x1, waiting for transfers between devices, on_device(): lax.all_to_all(replies, 'pts', split_axis=0, concat_axis=0, tiled=True)  19.8 us
    dot_general x14, matrix products, pair_costs(): jnp.einsum('gid,gjd->gij', source_rows, target_rows, preferred_element_ty...  19.8 us
    all_to_all x3, waiting for transfers between devices, on_device(): lax.all_to_all(out_masses, 'pts', split_axis=0, concat_axis=0, tiled=True)  18.6 us
    all_to_all x3, waiting for transfers between devices, on_device(): lax.all_to_all(out_peaks, 'pts', split_axis=0, concat_axis=0, tiled=True)  15.7 us
    all_to_all x1, blocking collectives, on_device(): lax.all_to_all(wanted, 'pts', split_axis=0, concat_axis=0, tiled=True)  15.4 us
    all_to_all x2, waiting for transfers between devices, on_device(): lax.all_to_all(returned, 'pts', split_axis=0, concat_axis=0, tiled=True)  12.8 us
    all_to_all x3, starting transfers between devices, on_device(): lax.all_to_all(out_peaks, 'pts', split_axis=0, concat_axis=0, tiled=True)  12.8 us
    all_to_all x1, waiting for transfers between devices, on_device(): lax.all_to_all(outgoing, 'pts', split_axis=0, concat_axis=0, tiled=True)  11.8 us
  transfers between devices with their start and end apart: 12, of which 12 were waited for; matrix products, arithmetic and copies ran while one was open for 9% of the time, Pallas kernels for 0%

commit v1 on v0

v1 whole, which is shorter than its diff:
```python
import functools

import jax
import jax.numpy as jnp
from jax import lax
from jax.experimental import pallas as pl
from jax.experimental.pallas import tpu as pltpu
from jax.sharding import PartitionSpec as P

BLOCK = 128
ITERS = 3
EPSILON = 0.05
NEG_BIG = -1e30
MESH = pl.DeviceIdType.MESH
VMEM_BYTES = 56 * 1024 * 1024


def loop(lower, upper, body):
    def step(i, carry):
        body(i)
        return carry

    lax.fori_loop(lower, upper, step, 0)


def grouped(total, size, body):
    def step(i):
        for k in range(size):
            body(i * size + k)

    loop(0, total // size, step)


def flipped(me, d, n):
    if n & (n - 1):
        return lax.rem(me + d, n)
    out, bit = 0, 1
    while bit < n:
        out = out + bit * (((me // bit) + (d // bit)) % 2)
        bit *= 2
    return out


def as_column(row):
    return jnp.transpose(jnp.broadcast_to(row, (BLOCK, BLOCK)))


def square_row(block):
    values = block.astype(jnp.float32)
    column = jnp.sum(values * values, axis=1, keepdims=True)
    return jnp.transpose(jnp.broadcast_to(column, (BLOCK, BLOCK)))[0:1, :]


def combine(peaks, masses, keys, key):
    member = keys == key
    top = jnp.max(jnp.where(member, peaks, NEG_BIG), axis=0, keepdims=True)
    parts = masses * jnp.exp(jnp.where(member, peaks - top, NEG_BIG))
    return top, jnp.sum(jnp.where(member, parts, 0.0), axis=0, keepdims=True)


def exchange_kernel(
    n, blocks, half, scale,
    source_pick, source_keys, want_rows, src_hbm, tgt_hbm,
    rx_out, ids_out, a_out, b_out, source_out, target_out,
    src, tgt, out_x, rx, score, score_t, b_col, ids_in, ids_all, ids_smem, id_keys,
    stats_out, stats_in, peak_rows, mass_rows, rep_out, rep_in, a_src, a_send, a_in, a_all, b_all,
    x_sq, y_sq,
    load_sem, x_send, x_recv, id_send, id_recv, fwd_send, fwd_recv, keep_sem,
    stat_send, stat_recv, a_ssem, a_rsem, rep_send, rep_recv, tail_send, tail_recv,
):
    me = lax.axis_index("pts")
    side = lax.axis_index("rep")
    other = 1 - side
    first = side * half

    load_src = pltpu.make_async_copy(src_hbm, src, load_sem.at[0])
    load_tgt = pltpu.make_async_copy(tgt_hbm, tgt, load_sem.at[1])
    load_src.start()
    load_tgt.start()

    barrier = pltpu.get_barrier_semaphore()

    def greet(d):
        pl.semaphore_signal(
            barrier, inc=1, device_id=(lax.rem(me + d, n), side), device_id_type=MESH
        )

    loop(1, n, greet)
    pl.semaphore_signal(barrier, inc=1, device_id=(me, other), device_id_type=MESH)
    pl.semaphore_wait(barrier, n)

    def to_peer(src_ref, dst_ref, send_sem, recv_sem, peer):
        return pltpu.make_async_remote_copy(
            src_ref=src_ref, dst_ref=dst_ref, send_sem=send_sem, recv_sem=recv_sem,
            device_id=(peer, side), device_id_type=MESH,
        )

    def to_twin(src_ref, dst_ref, send_sem, recv_sem):
        return pltpu.make_async_remote_copy(
            src_ref=src_ref, dst_ref=dst_ref, send_sem=send_sem, recv_sem=recv_sem,
            device_id=(me, other), device_id_type=MESH,
        )

    def id_copy(peer, slot):
        return to_peer(want_rows.at[peer], ids_in.at[slot], id_send.at[peer], id_recv.at[slot], peer)

    def x_copy(peer, slot):
        return to_peer(out_x.at[peer], rx.at[slot], x_send.at[peer], x_recv.at[slot], peer)

    def stat_copy(it, peer, slot):
        return to_peer(
            stats_out.at[it, peer], stats_in.at[it, slot],
            stat_send.at[it, peer], stat_recv.at[it, slot], peer,
        )

    def a_copy(it, peer, slot):
        return to_peer(
            a_send.at[it, peer], a_in.at[it, slot], a_ssem.at[it, peer], a_rsem.at[it, slot], peer
        )

    def keep_copy(slot):
        return pltpu.make_async_copy(rx.at[slot], rx_out.at[side, slot], keep_sem.at[slot])

    def forward_copy(slot, which):
        return to_twin(
            rx.at[slot], rx_out.at[which, slot], fwd_send.at[slot], fwd_recv.at[slot]
        )

    loop(1, n, lambda d: id_copy(lax.rem(me + d, n), me).start())
    load_src.wait()

    def send_block(d):
        peer = flipped(me, d, n)
        out_x[peer] = src[jnp.maximum(source_pick[peer], 0)]
        x_copy(peer, me).start()

    loop(n // 2, n, send_block)
    loop(1, n // 2, send_block)
    rx[me] = src[jnp.maximum(source_pick[me], 0)]
    ids_in[me] = want_rows[me]
    load_tgt.wait()

    def source_squares(b):
        x_sq[pl.ds(b, 1), :] = scale * square_row(src[b])

    def target_squares(b):
        row = scale * square_row(tgt[b])
        y_sq[b // half, pl.ds(b % half, 1), :] = row
        b_col[b] = as_column(-row)

    loop(0, blocks, source_squares)
    loop(0, blocks, target_squares)

    def take_id(d):
        peer = lax.rem(me + d, n)
        id_copy(peer, peer).wait_recv()

    loop(1, n, take_id)
    ids_move = pltpu.make_async_copy(ids_in, ids_smem, load_sem.at[2])
    ids_move.start()

    def id_row(q):
        row = ids_in[q]
        id_keys[pl.ds(q, 1), :] = row
        ids_all[side, pl.ds(q, 1), :] = row

    loop(0, n, id_row)
    ids_move.wait()

    def row_stats(it, q, local_target):
        terms = b_col[local_target] + score_t[q]
        top = jnp.max(terms, axis=0, keepdims=True)
        stats_out[it, q, 0:1, :] = top
        stats_out[it, q, 1:2, :] = jnp.sum(jnp.exp(terms - top), axis=0, keepdims=True)

    def local_id(q):
        return jnp.maximum(ids_smem[q, 0, 0], 0)

    def first_visit(q):
        keep_copy(q).start()
        forward_copy(q, side).start()
        pick = local_id(q)
        grid = lax.dot_general(
            rx[q], tgt[pick], (((1,), (1,)), ((), ())), preferred_element_type=jnp.float32
        ) * (2.0 * scale)
        grid_t = jnp.transpose(grid)
        score[q] = grid
        score_t[q] = grid_t
        terms = b_col[pick] + grid_t
        top = jnp.max(terms, axis=0, keepdims=True)
        stats_out[0, q, 0:1, :] = top
        stats_out[0, q, 1:2, :] = jnp.sum(jnp.exp(terms - top), axis=0, keepdims=True)

    def own_stats(it):
        stats_in[it, me] = stats_out[it, me]

    first_visit(me)
    own_stats(0)

    def arrival(d):
        peer = flipped(me, d, n)
        x_copy(peer, peer).wait_recv()
        first_visit(peer)
        stat_copy(0, peer, me).start()

    loop(n // 2, n, arrival)
    loop(1, n // 2, arrival)

    for it in range(ITERS):
        def take_stats(d):
            peer = lax.rem(me + d, n)
            stat_copy(it, peer, peer).wait_recv()

        loop(1, n, take_stats)

        def stat_row(p):
            peak_rows[pl.ds(p, 1), :] = stats_in[it, p, 0:1, :]
            mass_rows[pl.ds(p, 1), :] = stats_in[it, p, 1:2, :]

        grouped(n, 8, stat_row)
        peaks, masses, keys = peak_rows[...], mass_rows[...], source_keys[...]
        for b in range(blocks):
            top, total = combine(peaks, masses, keys, b)
            rep_out[it, 0, b:b + 1, :] = top
            rep_out[it, 1, b:b + 1, :] = total
        swap = to_twin(rep_out.at[it], rep_in.at[it], rep_send.at[it], rep_recv.at[it])
        swap.start()
        swap.wait_recv()
        top = jnp.maximum(rep_out[it, 0], rep_in[it, 0])
        total = rep_out[it, 1] * jnp.exp(rep_out[it, 0] - top) + rep_in[it, 1] * jnp.exp(
            rep_in[it, 0] - top
        )
        a_src[...] = -(top + jnp.log(total))

        def send_a(d):
            peer = lax.rem(me + d, n)
            a_send[it, peer] = a_src[pl.ds(jnp.maximum(source_pick[peer], 0), 1), :]
            a_copy(it, peer, me).start()

        loop(1, n, send_a)
        a_in[it, me] = a_src[pl.ds(jnp.maximum(source_pick[me], 0), 1), :]

        def take_a(d):
            peer = lax.rem(me + d, n)
            a_copy(it, peer, peer).wait_recv()

        loop(1, n, take_a)

        def column_visit(q):
            terms = as_column(a_in[it, q]) + score[q]
            top = jnp.max(terms, axis=0, keepdims=True)
            peak_rows[pl.ds(q, 1), :] = top
            mass_rows[pl.ds(q, 1), :] = jnp.sum(jnp.exp(terms - top), axis=0, keepdims=True)

        grouped(n, 4, column_visit)
        peaks, masses, keys = peak_rows[...], mass_rows[...], id_keys[...]
        for b in range(half):
            top, total = combine(peaks, masses, keys, b + first)
            row = -(top + jnp.log(total))
            if it + 1 < ITERS:
                b_col[first + b] = as_column(row)
            else:
                b_all[side, b:b + 1, :] = row

        if it + 1 < ITERS:
            grouped(n, 4, lambda q: row_stats(it + 1, q, local_id(q)))
            own_stats(it + 1)

            def send_stats(d):
                stat_copy(it + 1, lax.rem(me + d, n), me).start()

            loop(1, n, send_stats)

    def last_row(q):
        a_all[side, pl.ds(q, 1), :] = a_in[ITERS - 1, q]

    grouped(n, 8, last_row)
    tails = [
        to_twin(ref.at[side], ref.at[side], tail_send.at[k], tail_recv.at[k])
        for k, ref in enumerate((ids_all, a_all, b_all))
    ]
    for copy in tails:
        copy.start()
    source_out[...] = EPSILON * (a_src[...] + x_sq[...])

    def finish_local(q):
        keep_copy(q).wait()
        forward_copy(q, other).wait_recv()
        forward_copy(q, side).wait_send()

    loop(0, n, finish_local)

    def finish_sends(d):
        peer = lax.rem(me + d, n)
        id_copy(peer, me).wait_send()
        x_copy(peer, me).wait_send()
        for it in range(ITERS):
            stat_copy(it, peer, me).wait_send()
            a_copy(it, peer, me).wait_send()

    loop(1, n, finish_sends)
    for it in range(ITERS):
        to_twin(rep_out.at[it], rep_in.at[it], rep_send.at[it], rep_recv.at[it]).wait_send()
    for k, ref in enumerate((ids_all, a_all, b_all)):
        to_twin(ref.at[other], ref.at[other], tail_send.at[k], tail_recv.at[k]).wait_recv()
        tails[k].wait_send()
    ids_out[...] = ids_all[...]
    a_out[...] = a_all[...]
    b_out[...] = b_all[...]
    target_out[...] = EPSILON * (b_all[...] + y_sq[...])


def gradient_kernel(pairs, blocks, scale, ids, rx, a_rows, b_rows, tgt, grad, b_col, mass):
    def prepare(b):
        grad[b] = jnp.zeros(grad.shape[1:], jnp.float32)
        mass[b] = jnp.zeros((BLOCK, BLOCK), jnp.float32)
        b_col[b] = as_column(b_rows[pl.ds(b, 1), :])

    grouped(blocks, 4, prepare)

    def visit(k0):
        results = []
        for k in range(4):
            q = k0 * 4 + k
            target = ids[q, 0]
            pick = jnp.maximum(target, 0)
            grid = lax.dot_general(
                tgt[pick], rx[q], (((1,), (1,)), ((), ())), preferred_element_type=jnp.float32
            ) * (2.0 * scale)
            plan = jnp.exp(b_col[pick] + (grid + a_rows[pl.ds(q, 1), :]))
            plan = jnp.where(target >= 0, plan, 0.0)
            part = jnp.dot(plan.astype(jnp.bfloat16), rx[q], preferred_element_type=jnp.float32)
            results.append((pick, plan, part))
        for pick, plan, part in results:
            grad[pick] += part
            mass[pick] += plan

    loop(0, pairs // 4, visit)

    def finish(b):
        column = jnp.sum(mass[b], axis=1, keepdims=True)
        grad[b] = tgt[b].astype(jnp.float32) * column - grad[b]

    grouped(blocks, 2, finish)


def on_device(src_points, tgt_points, pair_source, pair_target, pair_count):
    n = lax.axis_size("pts")
    reps = lax.axis_size("rep")
    rows, dim = src_points.shape
    blocks = rows // BLOCK
    half = blocks // reps
    scale = 1.0 / EPSILON / dim
    src = src_points.reshape(blocks, BLOCK, dim)
    tgt = tgt_points.reshape(blocks, BLOCK, dim)
    usable = jnp.arange(pair_source.shape[0]) < pair_count[0]
    owner = pair_target // blocks
    matched = (owner[:, None] == jnp.arange(n)[None, :]) & usable[:, None]
    wanted = jnp.max(jnp.where(matched, (pair_target % blocks)[:, None], -1), axis=0)
    picked = jnp.max(jnp.where(matched, (pair_source % blocks)[:, None], -1), axis=0)
    source_keys = jnp.broadcast_to(picked[:, None], (n, BLOCK))
    want_rows = jnp.broadcast_to(wanted[:, None, None], (n, 1, BLOCK))

    f32, bf16, i32 = jnp.float32, jnp.bfloat16, jnp.int32
    shape = jax.ShapeDtypeStruct
    vmem = pl.BlockSpec(memory_space=pltpu.VMEM)
    smem = pl.BlockSpec(memory_space=pltpu.SMEM)
    hbm = pl.BlockSpec(memory_space=pl.ANY)
    dma = pltpu.SemaphoreType.DMA
    with jax.named_scope("exchange_and_sweeps"):
        rx, ids, a_rows, b_rows, source_dual, target_dual = pl.pallas_call(
            functools.partial(exchange_kernel, n, blocks, half, scale),
            out_shape=(
                shape((reps, n, BLOCK, dim), bf16),
                shape((reps, n, BLOCK), i32),
                shape((reps, n, BLOCK), f32),
                shape((reps, half, BLOCK), f32),
                shape((blocks, BLOCK), f32),
                shape((reps, half, BLOCK), f32),
            ),
            in_specs=[smem, vmem, vmem, hbm, hbm],
            out_specs=(hbm, vmem, vmem, vmem, vmem, vmem),
            scratch_shapes=[
                pltpu.VMEM((blocks, BLOCK, dim), bf16),
                pltpu.VMEM((blocks, BLOCK, dim), bf16),
                pltpu.VMEM((n, BLOCK, dim), bf16),
                pltpu.VMEM((n, BLOCK, dim), bf16),
                pltpu.VMEM((n, BLOCK, BLOCK), f32),
                pltpu.VMEM((n, BLOCK, BLOCK), f32),
                pltpu.VMEM((blocks, BLOCK, BLOCK), f32),
                pltpu.VMEM((n, 1, BLOCK), i32),
                pltpu.VMEM((reps, n, BLOCK), i32),
                pltpu.SMEM((n, 1, BLOCK), i32),
                pltpu.VMEM((n, BLOCK), i32),
                pltpu.VMEM((ITERS, n, 2, BLOCK), f32),
                pltpu.VMEM((ITERS, n, 2, BLOCK), f32),
                pltpu.VMEM((n, BLOCK), f32),
                pltpu.VMEM((n, BLOCK), f32),
                pltpu.VMEM((ITERS, 2, blocks, BLOCK), f32),
                pltpu.VMEM((ITERS, 2, blocks, BLOCK), f32),
                pltpu.VMEM((blocks, BLOCK), f32),
                pltpu.VMEM((ITERS, n, 1, BLOCK), f32),
                pltpu.VMEM((ITERS, n, 1, BLOCK), f32),
                pltpu.VMEM((reps, n, BLOCK), f32),
                pltpu.VMEM((reps, half, BLOCK), f32),
                pltpu.VMEM((blocks, BLOCK), f32),
                pltpu.VMEM((reps, half, BLOCK), f32),
                dma((3,)),
                dma((n,)), dma((n,)), dma((n,)), dma((n,)), dma((n,)), dma((n,)), dma((n,)),
                dma((ITERS, n)), dma((ITERS, n)), dma((ITERS, n)), dma((ITERS, n)),
                dma((ITERS,)), dma((ITERS,)), dma((3,)), dma((3,)),
            ],
            compiler_params=pltpu.CompilerParams(
                collective_id=0, has_side_effects=True, vmem_limit_bytes=VMEM_BYTES
            ),
            name="exchange_and_sweeps",
        )(picked, source_keys, want_rows, src, tgt)
    pairs = reps * n
    with jax.named_scope("gradient"):
        grad = pl.pallas_call(
            functools.partial(gradient_kernel, pairs, blocks, scale),
            out_shape=shape((blocks, BLOCK, dim), f32),
            in_specs=[smem, vmem, vmem, vmem, vmem],
            out_specs=vmem,
            scratch_shapes=[
                pltpu.VMEM((blocks, BLOCK, BLOCK), f32),
                pltpu.VMEM((blocks, BLOCK, BLOCK), f32),
            ],
            compiler_params=pltpu.CompilerParams(vmem_limit_bytes=VMEM_BYTES),
            name="gradient",
        )(
            ids.reshape(pairs, BLOCK),
            rx.reshape(pairs, BLOCK, dim),
            a_rows.reshape(pairs, BLOCK),
            b_rows.reshape(blocks, BLOCK),
            tgt,
        )
    return source_dual.reshape(-1), target_dual.reshape(-1), grad.reshape(rows, dim)


def solution(mesh):
    return jax.shard_map(
        on_device,
        mesh=mesh,
        in_specs=(
            P("pts", None),
            P("pts", None),
            P(("pts", "rep")),
            P(("pts", "rep")),
            P(("pts", "rep")),
        ),
        out_specs=(P("pts"), P("pts"), P("pts", None)),
        check_vma=False,
    )
```

time: 274 us -> 86 us (0.31)
  waiting for transfers between devices: 91.3 us -> 0 us
  Pallas kernels: 0 us -> 78.8 us
  starting transfers between devices: 43.6 us -> 0 us
  local copies, waits for them, and re-layouts: 37.8 us -> 4.6 us
  blocking collectives: 31.8 us -> 0 us
  other arithmetic: 27.5 us -> 0.79 us
  matrix products: 23.9 us -> 0 us
  between operations: 15.9 us -> 1.31 us
    all_to_all x11 -> x0, waiting for transfers between devices: 83.9 us -> none  [the longest x1 19.8 us: on_device(): lax.all_to_all(replies, 'pts', split_axis=0, concat_axis=0, tiled=True)]
    pallas_call x0 -> x2, Pallas kernels: none -> 78.8 us  [the longest x1 68.6 us: on_device(): pl.pallas_call(functools.partial(exchange_kernel, n, blocks, half, scale)...]
    all_to_all x11 -> x0, starting transfers between devices: 43.6 us -> none  [the longest x3 12.8 us: on_device(): lax.all_to_all(out_peaks, 'pts', split_axis=0, concat_axis=0, tiled=True)]
    dot_general x18 -> x0, matrix products: 23.9 us -> none  [the longest x14 19.8 us: pair_costs(): jnp.einsum('gid,gjd->gij', source_rows, target_rows, preferred_element_ty...]
    gather x22 -> x0, local copies, waits for them, and re-layouts: 18.2 us -> none  [the longest x1 2.03 us: on_device(): own_targets[jnp.maximum(asked_ids, 0)]]
    all_gather x9 -> x0, blocking collectives: 16.4 us -> none  [the longest x6 10.9 us: joined(): gathered = jax.tree.map(lambda a: lax.all_gather(a, axis), part)]
    all_to_all x1 -> x0, blocking collectives: 15.4 us -> none  [on_device(): lax.all_to_all(wanted, 'pts', split_axis=0, concat_axis=0, tiled=True)]
    lt x15 -> x1, other arithmetic: 9.07 us -> 0.01 us  [on_device(): usable = jnp.arange(pair_source.shape[0]) < pair_count[0]]
  transfers between devices with their start and end apart: 12 -> 0, of which waited for: 12 -> 0; matrix products, arithmetic and copies ran while one was open for 9% -> 0% of each run, Pallas kernels for 0% -> 0%
where the time goes in v1:
time: 86 us; the launch traced here: 85.5 us
  Pallas kernels  78.8 us (92%)
  local copies, waits for them, and re-layouts  4.6 us (5%)
  between operations  1.31 us (2%)
    pallas_call x1, Pallas kernels, on_device(): pl.pallas_call(functools.partial(exchange_kernel, n, blocks, half, scale)...  68.6 us
    pallas_call x1, Pallas kernels, on_device(): pl.pallas_call(functools.partial(gradient_kernel, pairs, blocks, scale),...  10.2 us

profile of v1, /device:TPU:0, one launch (start us, length us, event | category | flops | bytes accessed | tf_op | source)
XLA Modules:
  0.0 85.5 jit_solution(5012422211914883911)
XLA Ops:
  1.3 0.7 and_select_fusion.2
  2.0 0.1 select_reduce_fusion
  2.1 0.0 copy-start.1
  2.1 0.7 broadcast_in_dim.39.want_rows
  2.8 0.7 broadcast_in_dim.37.source_keys
  3.4 0.0 copy-done.1
  3.4 68.6 %exchange_and_sweeps.1 = (bf16[2,16,128,256]{3,2,1,0:T(8,128)(2,1)}, s32[2,16,128]{2,1,0:T(8,128)}, f32[2,16,128]{2,1,0:T(8,128)}, f32[2,12,128]{2,1,0:T(8,128)}...) custom-call(s32[16]{0:T(128)} %copy-done.1, s32[16,128]{1,0:T(8,128)} %broadcast_in_dim.37.source_keys, ...), custom_call_target="tpu_custom_call" | custom-call | tf_op jit(solution)/shard_map/exchange_and_sweeps/exchange_and_sweeps/pallas_call | solution.py:371
  72.1 1.3 %reshape.47 = f32[3072]{0:T(1024)} reshape(f32[2,12,128]{2,1,0:T(8,128)} %get-tuple-element.10) | data formatting | bytes 24576 | tf_op jit(solution)/shard_map/reshape | solution.py:438
  73.4 1.3 %reshape.51.b_rows = f32[24,128]{1,0:T(8,128)} reshape(f32[2,12,128]{2,1,0:T(8,128)} %get-tuple-element.14) | data formatting | bytes 24576 | tf_op jit(solution)/shard_map/gradient/reshape | solution.py:435
  74.7 0.0 copy-start
  74.7 10.2 %gradient.1 = f32[24,128,256]{2,1,0:T(8,128)} custom-call(s32[32,128]{1,0:T(8,128)} %bitcast.14, bf16[32,128,256]{2,1,0:T(8,128)(2,1)} %bitcast.12, f32[32,128]{1,0:T(8,128)} %bitcast.15, f32[24,128]{1,0:T(8,128)} %reshape.51.b_rows, bf16[24,128,256]{2,1,0:T(8,128)(2,1)} %bitcast.10), custom_call_target="tpu_custom_call" | custom-call | tf_op jit(solution)/shard_map/gradient/gradient/pallas_call | solution.py:420
  84.9 0.0 copy-done
  84.9 0.6 copy.10
  (1 shorter events, 0.0 us)
Async XLA Ops:
  2.1 1.4 %copy-start.1 = (s32[16]{0:T(128)}, s32[16]{0:T(128)S(1)}, u32[]{:S(2)}) copy-start(s32[16]{0:T(128)S(1)} %get-tuple-element.16.source_pick) | copy-start | bytes 196
  74.7 10.2 %copy-start = (f32[24,128]{1,0:T(8,128)S(1)}, f32[24,128]{1,0:T(8,128)}, u32[]{:S(2)}) copy-start(f32[24,128]{1,0:T(8,128)} %get-tuple-element.9) | copy-start | bytes 36868

commit v2 on v1

--- a/solution.py
+++ b/solution.py
@@ -45,6 +45,11 @@
     return jnp.transpose(jnp.broadcast_to(row, (BLOCK, BLOCK)))
 
 
+def columns_of(rows):
+    turned = jnp.transpose(rows)
+    return [jnp.broadcast_to(turned[:, k:k + 1], (BLOCK, BLOCK)) for k in range(rows.shape[0])]
+
+
 def square_row(block):
     values = block.astype(jnp.float32)
     column = jnp.sum(values * values, axis=1, keepdims=True)
@@ -60,13 +65,13 @@
 
 def exchange_kernel(
     n, blocks, half, scale,
-    source_pick, source_keys, want_rows, src_hbm, tgt_hbm,
+    source_pick, wanted, src_hbm, tgt_hbm,
     rx_out, ids_out, a_out, b_out, source_out, target_out,
-    src, tgt, out_x, rx, score, score_t, b_col, ids_in, ids_all, ids_smem, id_keys,
-    stats_out, stats_in, peak_rows, mass_rows, rep_out, rep_in, a_src, a_send, a_in, a_all, b_all,
-    x_sq, y_sq,
+    src, tgt, out_x, rx, score, score_t, b_col, want_rows, ids_in, ids_all, ids_smem, id_keys,
+    key_all, stats_out, stats_in, peak_rows, mass_rows, a_src, a_send, a_in, a_rows, a_all, b_all,
+    b_pad, x_sq, y_sq,
     load_sem, x_send, x_recv, id_send, id_recv, fwd_send, fwd_recv, keep_sem,
-    stat_send, stat_recv, a_ssem, a_rsem, rep_send, rep_recv, tail_send, tail_recv,
+    stat_send, stat_recv, a_ssem, a_rsem, tail_send, tail_recv,
 ):
     me = lax.axis_index("pts")
     side = lax.axis_index("rep")
@@ -85,9 +90,20 @@
             barrier, inc=1, device_id=(lax.rem(me + d, n), side), device_id_type=MESH
         )
 
+    def greet_other(d):
+        pl.semaphore_signal(
+            barrier, inc=1, device_id=(lax.rem(me + d, n), other), device_id_type=MESH
+        )
+
     loop(1, n, greet)
-    pl.semaphore_signal(barrier, inc=1, device_id=(me, other), device_id_type=MESH)
-    pl.semaphore_wait(barrier, n)
+    loop(0, n, greet_other)
+
+    def list_row(p):
+        want_rows[p] = jnp.full((1, BLOCK), wanted[p], jnp.int32)
+        key_all[side, pl.ds(p, 1), :] = jnp.full((1, BLOCK), source_pick[p], jnp.int32)
+
+    grouped(n, 8, list_row)
+    pl.semaphore_wait(barrier, 2 * n - 1)
 
     def to_peer(src_ref, dst_ref, send_sem, recv_sem, peer):
         return pltpu.make_async_remote_copy(
@@ -107,10 +123,11 @@
     def x_copy(peer, slot):
         return to_peer(out_x.at[peer], rx.at[slot], x_send.at[peer], x_recv.at[slot], peer)
 
-    def stat_copy(it, peer, slot):
-        return to_peer(
-            stats_out.at[it, peer], stats_in.at[it, slot],
-            stat_send.at[it, peer], stat_recv.at[it, slot], peer,
+    def stat_copy(it, peer, to_side, from_side, slot):
+        return pltpu.make_async_remote_copy(
+            src_ref=stats_out.at[it, peer], dst_ref=stats_in.at[it, from_side, slot],
+            send_sem=stat_send.at[it, to_side, peer], recv_sem=stat_recv.at[it, from_side, slot],
+            device_id=(peer, to_side), device_id_type=MESH,
         )
 
     def a_copy(it, peer, slot):
@@ -126,7 +143,11 @@
             rx.at[slot], rx_out.at[which, slot], fwd_send.at[slot], fwd_recv.at[slot]
         )
 
+    def tail_copy(k, ref, which):
+        return to_twin(ref.at[which], ref.at[which], tail_send.at[k], tail_recv.at[k])
+
     loop(1, n, lambda d: id_copy(lax.rem(me + d, n), me).start())
+    tail_copy(3, key_all, side).start()
     load_src.wait()
 
     def send_block(d):
@@ -139,13 +160,14 @@
     rx[me] = src[jnp.maximum(source_pick[me], 0)]
     ids_in[me] = want_rows[me]
     load_tgt.wait()
+    b_pad[...] = jnp.zeros(b_pad.shape, jnp.float32)
 
     def source_squares(b):
         x_sq[pl.ds(b, 1), :] = scale * square_row(src[b])
 
     def target_squares(b):
         row = scale * square_row(tgt[b])
-        y_sq[b // half, pl.ds(b % half, 1), :] = row
+        y_sq[pl.ds(b, 1), :] = row
         b_col[b] = as_column(-row)
 
     loop(0, blocks, source_squares)
@@ -165,6 +187,7 @@
         ids_all[side, pl.ds(q, 1), :] = row
 
     loop(0, n, id_row)
+    tail_copy(0, ids_all, side).start()
     ids_move.wait()
 
     def row_stats(it, q, local_target):
@@ -192,45 +215,43 @@
         stats_out[0, q, 1:2, :] = jnp.sum(jnp.exp(terms - top), axis=0, keepdims=True)
 
     def own_stats(it):
-        stats_in[it, me] = stats_out[it, me]
+        stats_in[it, side, me] = stats_out[it, me]
 
     first_visit(me)
     own_stats(0)
+    stat_copy(0, me, other, side, me).start()
 
     def arrival(d):
         peer = flipped(me, d, n)
         x_copy(peer, peer).wait_recv()
         first_visit(peer)
-        stat_copy(0, peer, me).start()
+        stat_copy(0, peer, other, side, me).start()
+        stat_copy(0, peer, side, side, me).start()
 
     loop(n // 2, n, arrival)
     loop(1, n // 2, arrival)
+    tail_copy(3, key_all, other).wait_recv()
 
     for it in range(ITERS):
         def take_stats(d):
             peer = lax.rem(me + d, n)
-            stat_copy(it, peer, peer).wait_recv()
-
+            stat_copy(it, peer, side, other, peer).wait_recv()
+            stat_copy(it, peer, side, side, peer).wait_recv()
+
+        stat_copy(it, me, side, other, me).wait_recv()
         loop(1, n, take_stats)
-
-        def stat_row(p):
-            peak_rows[pl.ds(p, 1), :] = stats_in[it, p, 0:1, :]
-            mass_rows[pl.ds(p, 1), :] = stats_in[it, p, 1:2, :]
-
-        grouped(n, 8, stat_row)
-        peaks, masses, keys = peak_rows[...], mass_rows[...], source_keys[...]
+        for part in range(2):
+            def stat_row(p):
+                peak_rows[part, pl.ds(p, 1), :] = stats_in[it, part, p, 0:1, :]
+                mass_rows[part, pl.ds(p, 1), :] = stats_in[it, part, p, 1:2, :]
+
+            grouped(n, 8, stat_row)
+        peaks = peak_rows[...].reshape(2 * n, BLOCK)
+        masses = mass_rows[...].reshape(2 * n, BLOCK)
+        keys = key_all[...].reshape(2 * n, BLOCK)
         for b in range(blocks):
             top, total = combine(peaks, masses, keys, b)
-            rep_out[it, 0, b:b + 1, :] = top
-            rep_out[it, 1, b:b + 1, :] = total
-        swap = to_twin(rep_out.at[it], rep_in.at[it], rep_send.at[it], rep_recv.at[it])
-        swap.start()
-        swap.wait_recv()
-        top = jnp.maximum(rep_out[it, 0], rep_in[it, 0])
-        total = rep_out[it, 1] * jnp.exp(rep_out[it, 0] - top) + rep_in[it, 1] * jnp.exp(
-            rep_in[it, 0] - top
-        )
-        a_src[...] = -(top + jnp.log(total))
+            a_src[b:b + 1, :] = -(top + jnp.log(total))
 
         def send_a(d):
             peer = lax.rem(me + d, n)
@@ -246,41 +267,52 @@
 
         loop(1, n, take_a)
 
-        def column_visit(q):
-            terms = as_column(a_in[it, q]) + score[q]
-            top = jnp.max(terms, axis=0, keepdims=True)
-            peak_rows[pl.ds(q, 1), :] = top
-            mass_rows[pl.ds(q, 1), :] = jnp.sum(jnp.exp(terms - top), axis=0, keepdims=True)
-
-        grouped(n, 4, column_visit)
-        peaks, masses, keys = peak_rows[...], mass_rows[...], id_keys[...]
+        def a_row(q):
+            a_rows[pl.ds(q, 1), :] = a_in[it, q]
+
+        grouped(n, 8, a_row)
+        if it + 1 == ITERS:
+            a_all[side] = a_rows[...]
+            tail_copy(1, a_all, side).start()
+
+        def column_visits(chunk):
+            base = chunk * 16
+            for k, column in enumerate(columns_of(a_rows[pl.ds(pl.multiple_of(base, 16), 16), :])):
+                terms = column + score[base + k]
+                top = jnp.max(terms, axis=0, keepdims=True)
+                peak_rows[0, pl.ds(base + k, 1), :] = top
+                mass_rows[0, pl.ds(base + k, 1), :] = jnp.sum(
+                    jnp.exp(terms - top), axis=0, keepdims=True
+                )
+
+        loop(0, n // 16, column_visits)
+        peaks, masses, keys = peak_rows[0], mass_rows[0], id_keys[...]
         for b in range(half):
             top, total = combine(peaks, masses, keys, b + first)
-            row = -(top + jnp.log(total))
-            if it + 1 < ITERS:
-                b_col[first + b] = as_column(row)
-            else:
-                b_all[side, b:b + 1, :] = row
-
-        if it + 1 < ITERS:
-            grouped(n, 4, lambda q: row_stats(it + 1, q, local_id(q)))
+            b_pad[b:b + 1, :] = -(top + jnp.log(total))
+        if it + 1 == ITERS:
+            b_all[side] = b_pad[0:half, :]
+        else:
+            for b, column in enumerate(columns_of(b_pad[...])[:half]):
+                b_col[first + b] = column
+
+            def next_rows(group):
+                for k in range(4):
+                    q = lax.rem(me + group * 4 + k, n)
+                    row_stats(it + 1, q, local_id(q))
+                for k in range(4):
+                    d = group * 4 + k
+                    q = lax.rem(me + d, n)
+                    stat_copy(it + 1, q, other, side, me).start()
+
+                    @pl.when(d > 0)
+                    def _():
+                        stat_copy(it + 1, q, side, side, me).start()
+
+            loop(0, n // 4, next_rows)
             own_stats(it + 1)
 
-            def send_stats(d):
-                stat_copy(it + 1, lax.rem(me + d, n), me).start()
-
-            loop(1, n, send_stats)
-
-    def last_row(q):
-        a_all[side, pl.ds(q, 1), :] = a_in[ITERS - 1, q]
-
-    grouped(n, 8, last_row)
-    tails = [
-        to_twin(ref.at[side], ref.at[side], tail_send.at[k], tail_recv.at[k])
-        for k, ref in enumerate((ids_all, a_all, b_all))
-    ]
-    for copy in tails:
-        copy.start()
+    tail_copy(2, b_all, side).start()
     source_out[...] = EPSILON * (a_src[...] + x_sq[...])
 
     def finish_local(q):
@@ -295,33 +327,51 @@
         id_copy(peer, me).wait_send()
         x_copy(peer, me).wait_send()
         for it in range(ITERS):
-            stat_copy(it, peer, me).wait_send()
+            stat_copy(it, peer, other, side, me).wait_send()
+            stat_copy(it, peer, side, side, me).wait_send()
             a_copy(it, peer, me).wait_send()
 
     loop(1, n, finish_sends)
     for it in range(ITERS):
-        to_twin(rep_out.at[it], rep_in.at[it], rep_send.at[it], rep_recv.at[it]).wait_send()
+        stat_copy(it, me, other, side, me).wait_send()
+    tail_copy(3, key_all, side).wait_send()
     for k, ref in enumerate((ids_all, a_all, b_all)):
-        to_twin(ref.at[other], ref.at[other], tail_send.at[k], tail_recv.at[k]).wait_recv()
-        tails[k].wait_send()
+        tail_copy(k, ref, other).wait_recv()
+        tail_copy(k, ref, side).wait_send()
     ids_out[...] = ids_all[...]
     a_out[...] = a_all[...]
-    b_out[...] = b_all[...]
-    target_out[...] = EPSILON * (b_all[...] + y_sq[...])
-
-
-def gradient_kernel(pairs, blocks, scale, ids, rx, a_rows, b_rows, tgt, grad, b_col, mass):
+    for part in range(2):
+        b_out[part * half:(part + 1) * half, :] = b_all[part]
+    target_out[...] = EPSILON * (b_out[...] + y_sq[...])
+
+
+def gradient_kernel(
+    pairs, blocks, scale, ids, rx_hbm, a_rows, b_rows, tgt, out, rx, grad, b_col, mass, sems, out_sems
+):
+    groups = pairs // 4
+
+    def fetch(group):
+        part = pl.ds(group * 4, 4)
+        return pltpu.make_async_copy(rx_hbm.at[part], rx.at[part], sems.at[group])
+
+    def store(b):
+        return pltpu.make_async_copy(grad.at[b], out.at[b], out_sems.at[b])
+
+    loop(0, groups, lambda group: fetch(group).start())
+    for b, column in enumerate(columns_of(b_rows[...])):
+        b_col[b] = column
+
     def prepare(b):
         grad[b] = jnp.zeros(grad.shape[1:], jnp.float32)
         mass[b] = jnp.zeros((BLOCK, BLOCK), jnp.float32)
-        b_col[b] = as_column(b_rows[pl.ds(b, 1), :])
 
     grouped(blocks, 4, prepare)
 
-    def visit(k0):
+    def visit(group):
+        fetch(group).wait()
         results = []
         for k in range(4):
-            q = k0 * 4 + k
+            q = group * 4 + k
             target = ids[q, 0]
             pick = jnp.maximum(target, 0)
             grid = lax.dot_general(
@@ -335,13 +385,18 @@
             grad[pick] += part
             mass[pick] += plan
 
-    loop(0, pairs // 4, visit)
-
-    def finish(b):
-        column = jnp.sum(mass[b], axis=1, keepdims=True)
-        grad[b] = tgt[b].astype(jnp.float32) * column - grad[b]
-
-    grouped(blocks, 2, finish)
+    loop(0, groups, visit)
+
+    def finish(group):
+        for k in range(4):
+            b = group * 4 + k
+            column = jnp.sum(mass[b], axis=1, keepdims=True)
+            grad[b] = tgt[b].astype(jnp.float32) * column - grad[b]
+        for k in range(4):
+            store(group * 4 + k).start()
+
+    loop(0, blocks // 4, finish)
+    loop(0, blocks, lambda b: store(b).wait())
 
 
 def on_device(src_points, tgt_points, pair_source, pair_target, pair_count):
@@ -358,8 +413,6 @@
     matched = (owner[:, None] == jnp.arange(n)[None, :]) & usable[:, None]
     wanted = jnp.max(jnp.where(matched, (pair_target % blocks)[:, None], -1), axis=0)
     picked = jnp.max(jnp.where(matched, (pair_source % blocks)[:, None], -1), axis=0)
-    source_keys = jnp.broadcast_to(picked[:, None], (n, BLOCK))
-    want_rows = jnp.broadcast_to(wanted[:, None, None], (n, 1, BLOCK))
 
     f32, bf16, i32 = jnp.float32, jnp.bfloat16, jnp.int32
     shape = jax.ShapeDtypeStruct
@@ -374,11 +427,11 @@
                 shape((reps, n, BLOCK, dim), bf16),
                 shape((reps, n, BLOCK), i32),
                 shape((reps, n, BLOCK), f32),
-                shape((reps, half, BLOCK), f32),
                 shape((blocks, BLOCK), f32),
-                shape((reps, half, BLOCK), f32),
+                shape((blocks, BLOCK), f32),
+                shape((blocks, BLOCK), f32),
             ),
-            in_specs=[smem, vmem, vmem, hbm, hbm],
+            in_specs=[smem, smem, hbm, hbm],
             out_specs=(hbm, vmem, vmem, vmem, vmem, vmem),
             scratch_shapes=[
                 pltpu.VMEM((blocks, BLOCK, dim), bf16),
@@ -389,42 +442,48 @@
                 pltpu.VMEM((n, BLOCK, BLOCK), f32),
                 pltpu.VMEM((blocks, BLOCK, BLOCK), f32),
                 pltpu.VMEM((n, 1, BLOCK), i32),
+                pltpu.VMEM((n, 1, BLOCK), i32),
                 pltpu.VMEM((reps, n, BLOCK), i32),
                 pltpu.SMEM((n, 1, BLOCK), i32),
                 pltpu.VMEM((n, BLOCK), i32),
+                pltpu.VMEM((reps, n, BLOCK), i32),
                 pltpu.VMEM((ITERS, n, 2, BLOCK), f32),
-                pltpu.VMEM((ITERS, n, 2, BLOCK), f32),
-                pltpu.VMEM((n, BLOCK), f32),
-                pltpu.VMEM((n, BLOCK), f32),
-                pltpu.VMEM((ITERS, 2, blocks, BLOCK), f32),
-                pltpu.VMEM((ITERS, 2, blocks, BLOCK), f32),
+                pltpu.VMEM((ITERS, reps, n, 2, BLOCK), f32),
+                pltpu.VMEM((reps, n, BLOCK), f32),
+                pltpu.VMEM((reps, n, BLOCK), f32),
                 pltpu.VMEM((blocks, BLOCK), f32),
                 pltpu.VMEM((ITERS, n, 1, BLOCK), f32),
                 pltpu.VMEM((ITERS, n, 1, BLOCK), f32),
+                pltpu.VMEM((n, BLOCK), f32),
                 pltpu.VMEM((reps, n, BLOCK), f32),
                 pltpu.VMEM((reps, half, BLOCK), f32),
+                pltpu.VMEM((-(-half // 8) * 8, BLOCK), f32),
                 pltpu.VMEM((blocks, BLOCK), f32),
-                pltpu.VMEM((reps, half, BLOCK), f32),
+                pltpu.VMEM((blocks, BLOCK), f32),
                 dma((3,)),
                 dma((n,)), dma((n,)), dma((n,)), dma((n,)), dma((n,)), dma((n,)), dma((n,)),
-                dma((ITERS, n)), dma((ITERS, n)), dma((ITERS, n)), dma((ITERS, n)),
-                dma((ITERS,)), dma((ITERS,)), dma((3,)), dma((3,)),
+                dma((ITERS, reps, n)), dma((ITERS, reps, n)), dma((ITERS, n)), dma((ITERS, n)),
+                dma((4,)), dma((4,)),
             ],
             compiler_params=pltpu.CompilerParams(
                 collective_id=0, has_side_effects=True, vmem_limit_bytes=VMEM_BYTES
             ),
             name="exchange_and_sweeps",
-        )(picked, source_keys, want_rows, src, tgt)
+        )(picked, wanted, src, tgt)
     pairs = reps * n
     with jax.named_scope("gradient"):
         grad = pl.pallas_call(
             functools.partial(gradient_kernel, pairs, blocks, scale),
             out_shape=shape((blocks, BLOCK, dim), f32),
-            in_specs=[smem, vmem, vmem, vmem, vmem],
-            out_specs=vmem,
+            in_specs=[smem, hbm, vmem, vmem, vmem],
+            out_specs=hbm,
             scratch_shapes=[
+                pltpu.VMEM((pairs, BLOCK, dim), bf16),
+                pltpu.VMEM((blocks, BLOCK, dim), f32),
                 pltpu.VMEM((blocks, BLOCK, BLOCK), f32),
                 pltpu.VMEM((blocks, BLOCK, BLOCK), f32),
+                dma((pairs // 4,)),
+                dma((blocks,)),
             ],
             compiler_params=pltpu.CompilerParams(vmem_limit_bytes=VMEM_BYTES),
             name="gradient",
@@ -432,7 +491,7 @@
             ids.reshape(pairs, BLOCK),
             rx.reshape(pairs, BLOCK, dim),
             a_rows.reshape(pairs, BLOCK),
-            b_rows.reshape(blocks, BLOCK),
+            b_rows,
             tgt,
         )
     return source_dual.reshape(-1), target_dual.reshape(-1), grad.reshape(rows, dim)

time: 86 us -> 83 us (0.965)
  local copies, waits for them, and re-layouts: 4.6 us -> 1.21 us
    reshape x2 -> x0, local copies, waits for them, and re-layouts: 2.64 us -> none  [the longest x1 1.32 us: on_device(): target_dual.reshape(-1)]
    pallas_call x1, Pallas kernels: 68.6 us -> 70.1 us  [on_device(): pl.pallas_call(functools.partial(exchange_kernel, n, blocks, half, scale)...]
    pallas_call x1, Pallas kernels: 10.2 us -> 8.86 us  [on_device(): pl.pallas_call(functools.partial(gradient_kernel, pairs, blocks, scale),...]
    broadcast_in_dim x2 -> x0, local copies, waits for them, and re-layouts: 1.35 us -> none  [the longest x1 0.68 us: on_device(): want_rows = jnp.broadcast_to(wanted[:, None, None], (n, 1, BLOCK))]
where the time goes in v2:
time: 83 us; the launch traced here: 82.8 us
  Pallas kernels  78.9 us (95%)
  between operations  1.33 us (2%)
  other arithmetic  1.3 us (2%)
  local copies, waits for them, and re-layouts  1.21 us (1%)
    pallas_call x1, Pallas kernels, on_device(): pl.pallas_call(functools.partial(exchange_kernel, n, blocks, half, scale)...  70.1 us
    pallas_call x1, Pallas kernels, on_device(): pl.pallas_call(functools.partial(gradient_kernel, pairs, blocks, scale),...  8.86 us

profile of v2, /device:TPU:0, one launch (start us, length us, event | category | flops | bytes accessed | tf_op | source)
XLA Modules:
  0.0 82.8 jit_solution(8011127971023176461)
XLA Ops:
  1.3 0.7 and_select_fusion.2
  2.0 0.6 select_reduce_fusion
  2.6 70.1 %exchange_and_sweeps.1 = (bf16[2,16,128,256]{3,2,1,0:T(8,128)(2,1)}, s32[2,16,128]{2,1,0:T(8,128)}, f32[2,16,128]{2,1,0:T(8,128)}, f32[24,128]{1,0:T(8,128)}, f32[24,128]{1,0:T(8,128)}, /*index=5*/f32[24,128]{1,0:T(8,128)}) custom-call(s32[16]{0:T(128)} %get-tuple-element.16.source_pick, s32[16]{0:T(128)} %get-tuple-element.15.wanted, ...), custom_call_target="tpu_custom_call" | custom-call | tf_op jit(solution)/shard_map/exchange_and_sweeps/exchange_and_sweeps/pallas_call | solution.py:424
  72.7 0.0 copy-start.1
  72.7 0.0 copy-start
  72.7 8.9 %gradient.1 = f32[24,128,256]{2,1,0:T(8,128)} custom-call(s32[32,128]{1,0:T(8,128)} %bitcast.15, bf16[32,128,256]{2,1,0:T(8,128)(2,1)} %bitcast.13, f32[32,128]{1,0:T(8,128)} %bitcast.16, f32[24,128]{1,0:T(8,128)} %get-tuple-element.14.b_rows, bf16[24,128,256]{2,1,0:T(8,128)(2,1)} %bitcast.11), custom_call_target="tpu_custom_call" | custom-call | tf_op jit(solution)/shard_map/gradient/gradient/pallas_call | solution.py:475
  81.6 0.0 copy-done.1
  81.6 0.6 copy.11
  82.2 0.0 copy-done
  82.2 0.6 copy.12
  (1 shorter events, 0.0 us)
Async XLA Ops:
  72.7 8.9 %copy-start.1 = (f32[24,128]{1,0:T(8,128)S(1)}, f32[24,128]{1,0:T(8,128)}, u32[]{:S(2)}) copy-start(f32[24,128]{1,0:T(8,128)} %get-tuple-element.9) | copy-start | bytes 36868
  72.7 9.5 %copy-start = (f32[24,128]{1,0:T(8,128)S(1)}, f32[24,128]{1,0:T(8,128)}, u32[]{:S(2)}) copy-start(f32[24,128]{1,0:T(8,128)} %get-tuple-element.10) | copy-start | bytes 36868

commit v3 on v2

--- a/solution.py
+++ b/solution.py
@@ -56,22 +56,28 @@
     return jnp.transpose(jnp.broadcast_to(column, (BLOCK, BLOCK)))[0:1, :]
 
 
-def combine(peaks, masses, keys, key):
-    member = keys == key
-    top = jnp.max(jnp.where(member, peaks, NEG_BIG), axis=0, keepdims=True)
-    parts = masses * jnp.exp(jnp.where(member, peaks - top, NEG_BIG))
-    return top, jnp.sum(jnp.where(member, parts, 0.0), axis=0, keepdims=True)
+def logsum(terms):
+    top = jnp.max(terms, axis=0, keepdims=True)
+    return top + jnp.log(jnp.sum(jnp.exp(terms - top), axis=0, keepdims=True))
+
+
+def combine(values, keys, key):
+    return logsum(jnp.where(keys == key, values, NEG_BIG))
+
+
+def in_turn(t, n):
+    return jnp.where(t % 2 == 0, n // 2 + t // 2, lax.rem((t + 1) // 2, n // 2))
 
 
 def exchange_kernel(
     n, blocks, half, scale,
-    source_pick, wanted, src_hbm, tgt_hbm,
+    pair_source, pair_target, pair_count, src_hbm, tgt_hbm,
     rx_out, ids_out, a_out, b_out, source_out, target_out,
     src, tgt, out_x, rx, score, score_t, b_col, want_rows, ids_in, ids_all, ids_smem, id_keys,
-    key_all, stats_out, stats_in, peak_rows, mass_rows, a_src, a_send, a_in, a_rows, a_all, b_all,
+    source_pick, wanted, source_keys, stats_out, stats_in, stat_rows, rep_out, rep_in, a_src, a_send, a_in, a_rows, a_all, b_all,
     b_pad, x_sq, y_sq,
     load_sem, x_send, x_recv, id_send, id_recv, fwd_send, fwd_recv, keep_sem,
-    stat_send, stat_recv, a_ssem, a_rsem, tail_send, tail_recv,
+    stat_send, stat_recv, a_ssem, a_rsem, rep_send, rep_recv, tail_send, tail_recv,
 ):
     me = lax.axis_index("pts")
     side = lax.axis_index("rep")
@@ -90,20 +96,31 @@
             barrier, inc=1, device_id=(lax.rem(me + d, n), side), device_id_type=MESH
         )
 
-    def greet_other(d):
-        pl.semaphore_signal(
-            barrier, inc=1, device_id=(lax.rem(me + d, n), other), device_id_type=MESH
-        )
-
     loop(1, n, greet)
-    loop(0, n, greet_other)
+    pl.semaphore_signal(barrier, inc=1, device_id=(me, other), device_id_type=MESH)
+
+    slots = pair_source.shape[0]
+    count = pair_count[0]
 
     def list_row(p):
-        want_rows[p] = jnp.full((1, BLOCK), wanted[p], jnp.int32)
-        key_all[side, pl.ds(p, 1), :] = jnp.full((1, BLOCK), source_pick[p], jnp.int32)
-
-    grouped(n, 8, list_row)
-    pl.semaphore_wait(barrier, 2 * n - 1)
+        def look(k, found):
+            offset = pair_target[k] - p * blocks
+            mine = (k < count) & (offset >= 0) & (offset < blocks)
+            local_source = pair_source[k] - me * blocks
+            return jnp.where(mine, local_source, found[0]), jnp.where(mine, offset, found[1])
+
+        found = (jnp.int32(-1), jnp.int32(-1))
+        if slots <= 16:
+            for k in range(slots):
+                found = look(k, found)
+        else:
+            found = lax.fori_loop(0, slots, look, found)
+        source_pick[p], wanted[p] = found
+        want_rows[p] = jnp.full((1, BLOCK), found[1], jnp.int32)
+        source_keys[pl.ds(p, 1), :] = jnp.full((1, BLOCK), found[0], jnp.int32)
+
+    loop(0, n, list_row)
+    pl.semaphore_wait(barrier, n)
 
     def to_peer(src_ref, dst_ref, send_sem, recv_sem, peer):
         return pltpu.make_async_remote_copy(
@@ -123,12 +140,14 @@
     def x_copy(peer, slot):
         return to_peer(out_x.at[peer], rx.at[slot], x_send.at[peer], x_recv.at[slot], peer)
 
-    def stat_copy(it, peer, to_side, from_side, slot):
-        return pltpu.make_async_remote_copy(
-            src_ref=stats_out.at[it, peer], dst_ref=stats_in.at[it, from_side, slot],
-            send_sem=stat_send.at[it, to_side, peer], recv_sem=stat_recv.at[it, from_side, slot],
-            device_id=(peer, to_side), device_id_type=MESH,
-        )
+    def stat_copy(it, peer, slot):
+        return to_peer(
+            stats_out.at[it, peer], stats_in.at[it, slot],
+            stat_send.at[it, peer], stat_recv.at[it, slot], peer,
+        )
+
+    def swap(it):
+        return to_twin(rep_out.at[it], rep_in.at[it], rep_send.at[it], rep_recv.at[it])
 
     def a_copy(it, peer, slot):
         return to_peer(
@@ -147,7 +166,6 @@
         return to_twin(ref.at[which], ref.at[which], tail_send.at[k], tail_recv.at[k])
 
     loop(1, n, lambda d: id_copy(lax.rem(me + d, n), me).start())
-    tail_copy(3, key_all, side).start()
     load_src.wait()
 
     def send_block(d):
@@ -155,8 +173,7 @@
         out_x[peer] = src[jnp.maximum(source_pick[peer], 0)]
         x_copy(peer, me).start()
 
-    loop(n // 2, n, send_block)
-    loop(1, n // 2, send_block)
+    loop(0, n - 1, lambda t: send_block(in_turn(t, n)))
     rx[me] = src[jnp.maximum(source_pick[me], 0)]
     ids_in[me] = want_rows[me]
     load_tgt.wait()
@@ -190,68 +207,57 @@
     tail_copy(0, ids_all, side).start()
     ids_move.wait()
 
-    def row_stats(it, q, local_target):
-        terms = b_col[local_target] + score_t[q]
-        top = jnp.max(terms, axis=0, keepdims=True)
-        stats_out[it, q, 0:1, :] = top
-        stats_out[it, q, 1:2, :] = jnp.sum(jnp.exp(terms - top), axis=0, keepdims=True)
-
     def local_id(q):
         return jnp.maximum(ids_smem[q, 0, 0], 0)
 
-    def first_visit(q):
-        keep_copy(q).start()
-        forward_copy(q, side).start()
-        pick = local_id(q)
-        grid = lax.dot_general(
-            rx[q], tgt[pick], (((1,), (1,)), ((), ())), preferred_element_type=jnp.float32
-        ) * (2.0 * scale)
-        grid_t = jnp.transpose(grid)
-        score[q] = grid
-        score_t[q] = grid_t
-        terms = b_col[pick] + grid_t
-        top = jnp.max(terms, axis=0, keepdims=True)
-        stats_out[0, q, 0:1, :] = top
-        stats_out[0, q, 1:2, :] = jnp.sum(jnp.exp(terms - top), axis=0, keepdims=True)
-
-    def own_stats(it):
-        stats_in[it, side, me] = stats_out[it, me]
-
-    first_visit(me)
-    own_stats(0)
-    stat_copy(0, me, other, side, me).start()
-
-    def arrival(d):
-        peer = flipped(me, d, n)
-        x_copy(peer, peer).wait_recv()
-        first_visit(peer)
-        stat_copy(0, peer, other, side, me).start()
-        stat_copy(0, peer, side, side, me).start()
-
-    loop(n // 2, n, arrival)
-    loop(1, n // 2, arrival)
-    tail_copy(3, key_all, other).wait_recv()
+    def arrivals(group):
+        offsets = [in_turn(group * 4 + k, n) for k in range(4)]
+        peers = [flipped(me, d, n) for d in offsets]
+        for d, peer in zip(offsets, peers):
+            @pl.when(d > 0)
+            def _():
+                x_copy(peer, peer).wait_recv()
+
+        for peer in peers:
+            pick = local_id(peer)
+            grid = lax.dot_general(
+                rx[peer], tgt[pick], (((1,), (1,)), ((), ())), preferred_element_type=jnp.float32
+            ) * (2.0 * scale)
+            grid_t = jnp.transpose(grid)
+            score[peer] = grid
+            score_t[peer] = grid_t
+            stats_out[0, peer] = logsum(b_col[pick] + grid_t)
+        for d, peer in zip(offsets, peers):
+            @pl.when(d > 0)
+            def _():
+                stat_copy(0, peer, me).start()
+
+        for peer in peers:
+            keep_copy(peer).start()
+            forward_copy(peer, side).start()
+
+    loop(0, n // 4, arrivals)
 
     for it in range(ITERS):
         def take_stats(d):
             peer = lax.rem(me + d, n)
-            stat_copy(it, peer, side, other, peer).wait_recv()
-            stat_copy(it, peer, side, side, peer).wait_recv()
-
-        stat_copy(it, me, side, other, me).wait_recv()
+            stat_copy(it, peer, peer).wait_recv()
+
         loop(1, n, take_stats)
-        for part in range(2):
-            def stat_row(p):
-                peak_rows[part, pl.ds(p, 1), :] = stats_in[it, part, p, 0:1, :]
-                mass_rows[part, pl.ds(p, 1), :] = stats_in[it, part, p, 1:2, :]
-
-            grouped(n, 8, stat_row)
-        peaks = peak_rows[...].reshape(2 * n, BLOCK)
-        masses = mass_rows[...].reshape(2 * n, BLOCK)
-        keys = key_all[...].reshape(2 * n, BLOCK)
+        stats_in[it, me] = stats_out[it, me]
+
+        def stat_row(p):
+            stat_rows[pl.ds(p, 1), :] = stats_in[it, p]
+
+        grouped(n, 8, stat_row)
+        values, keys = stat_rows[...], source_keys[...]
         for b in range(blocks):
-            top, total = combine(peaks, masses, keys, b)
-            a_src[b:b + 1, :] = -(top + jnp.log(total))
+            rep_out[it, b:b + 1, :] = combine(values, keys, b)
+        swap(it).start()
+        swap(it).wait_recv()
+        top = jnp.maximum(rep_out[it], rep_in[it])
+        total = jnp.exp(rep_out[it] - top) + jnp.exp(rep_in[it] - top)
+        a_src[...] = -(top + jnp.log(total))
 
         def send_a(d):
             peer = lax.rem(me + d, n)
@@ -278,18 +284,12 @@
         def column_visits(chunk):
             base = chunk * 16
             for k, column in enumerate(columns_of(a_rows[pl.ds(pl.multiple_of(base, 16), 16), :])):
-                terms = column + score[base + k]
-                top = jnp.max(terms, axis=0, keepdims=True)
-                peak_rows[0, pl.ds(base + k, 1), :] = top
-                mass_rows[0, pl.ds(base + k, 1), :] = jnp.sum(
-                    jnp.exp(terms - top), axis=0, keepdims=True
-                )
+                stat_rows[pl.ds(base + k, 1), :] = logsum(column + score[base + k])
 
         loop(0, n // 16, column_visits)
-        peaks, masses, keys = peak_rows[0], mass_rows[0], id_keys[...]
+        values, keys = stat_rows[...], id_keys[...]
         for b in range(half):
-            top, total = combine(peaks, masses, keys, b + first)
-            b_pad[b:b + 1, :] = -(top + jnp.log(total))
+            b_pad[b:b + 1, :] = -combine(values, keys, b + first)
         if it + 1 == ITERS:
             b_all[side] = b_pad[0:half, :]
         else:
@@ -299,18 +299,15 @@
             def next_rows(group):
                 for k in range(4):
                     q = lax.rem(me + group * 4 + k, n)
-                    row_stats(it + 1, q, local_id(q))
+                    stats_out[it + 1, q] = logsum(b_col[local_id(q)] + score_t[q])
                 for k in range(4):
                     d = group * 4 + k
-                    q = lax.rem(me + d, n)
-                    stat_copy(it + 1, q, other, side, me).start()
 
                     @pl.when(d > 0)
                     def _():
-                        stat_copy(it + 1, q, side, side, me).start()
+                        stat_copy(it + 1, lax.rem(me + d, n), me).start()
 
             loop(0, n // 4, next_rows)
-            own_stats(it + 1)
 
     tail_copy(2, b_all, side).start()
     source_out[...] = EPSILON * (a_src[...] + x_sq[...])
@@ -327,14 +324,12 @@
         id_copy(peer, me).wait_send()
         x_copy(peer, me).wait_send()
         for it in range(ITERS):
-            stat_copy(it, peer, other, side, me).wait_send()
-            stat_copy(it, peer, side, side, me).wait_send()
+            stat_copy(it, peer, me).wait_send()
             a_copy(it, peer, me).wait_send()
 
     loop(1, n, finish_sends)
     for it in range(ITERS):
-        stat_copy(it, me, other, side, me).wait_send()
-    tail_copy(3, key_all, side).wait_send()
+        swap(it).wait_send()
     for k, ref in enumerate((ids_all, a_all, b_all)):
         tail_copy(k, ref, other).wait_recv()
         tail_copy(k, ref, side).wait_send()
@@ -346,7 +341,8 @@
 
 
 def gradient_kernel(
-    pairs, blocks, scale, ids, rx_hbm, a_rows, b_rows, tgt, out, rx, grad, b_col, mass, sems, out_sems
+    pairs, blocks, scale, ids, rx_hbm, a_rows, b_rows, tgt, source_in, target_in,
+    out, source_out, target_out, rx, grad, b_col, mass, sems, out_sems,
 ):
     groups = pairs // 4
 
@@ -358,6 +354,8 @@
         return pltpu.make_async_copy(grad.at[b], out.at[b], out_sems.at[b])
 
     loop(0, groups, lambda group: fetch(group).start())
+    source_out[...] = source_in[...]
+    target_out[...] = target_in[...]
     for b, column in enumerate(columns_of(b_rows[...])):
         b_col[b] = column
 
@@ -408,11 +406,6 @@
     scale = 1.0 / EPSILON / dim
     src = src_points.reshape(blocks, BLOCK, dim)
     tgt = tgt_points.reshape(blocks, BLOCK, dim)
-    usable = jnp.arange(pair_source.shape[0]) < pair_count[0]
-    owner = pair_target // blocks
-    matched = (owner[:, None] == jnp.arange(n)[None, :]) & usable[:, None]
-    wanted = jnp.max(jnp.where(matched, (pair_target % blocks)[:, None], -1), axis=0)
-    picked = jnp.max(jnp.where(matched, (pair_source % blocks)[:, None], -1), axis=0)
 
     f32, bf16, i32 = jnp.float32, jnp.bfloat16, jnp.int32
     shape = jax.ShapeDtypeStruct
@@ -431,7 +424,7 @@
                 shape((blocks, BLOCK), f32),
                 shape((blocks, BLOCK), f32),
             ),
-            in_specs=[smem, smem, hbm, hbm],
+            in_specs=[smem, smem, smem, hbm, hbm],
             out_specs=(hbm, vmem, vmem, vmem, vmem, vmem),
             scratch_shapes=[
                 pltpu.VMEM((blocks, BLOCK, dim), bf16),
@@ -446,11 +439,14 @@
                 pltpu.VMEM((reps, n, BLOCK), i32),
                 pltpu.SMEM((n, 1, BLOCK), i32),
                 pltpu.VMEM((n, BLOCK), i32),
-                pltpu.VMEM((reps, n, BLOCK), i32),
-                pltpu.VMEM((ITERS, n, 2, BLOCK), f32),
-                pltpu.VMEM((ITERS, reps, n, 2, BLOCK), f32),
-                pltpu.VMEM((reps, n, BLOCK), f32),
-                pltpu.VMEM((reps, n, BLOCK), f32),
+                pltpu.SMEM((n,), i32),
+                pltpu.SMEM((n,), i32),
+                pltpu.VMEM((n, BLOCK), i32),
+                pltpu.VMEM((ITERS, n, 1, BLOCK), f32),
+                pltpu.VMEM((ITERS, n, 1, BLOCK), f32),
+                pltpu.VMEM((n, BLOCK), f32),
+                pltpu.VMEM((ITERS, blocks, BLOCK), f32),
+                pltpu.VMEM((ITERS, blocks, BLOCK), f32),
                 pltpu.VMEM((blocks, BLOCK), f32),
                 pltpu.VMEM((ITERS, n, 1, BLOCK), f32),
                 pltpu.VMEM((ITERS, n, 1, BLOCK), f32),
@@ -462,21 +458,25 @@
                 pltpu.VMEM((blocks, BLOCK), f32),
                 dma((3,)),
                 dma((n,)), dma((n,)), dma((n,)), dma((n,)), dma((n,)), dma((n,)), dma((n,)),
-                dma((ITERS, reps, n)), dma((ITERS, reps, n)), dma((ITERS, n)), dma((ITERS, n)),
-                dma((4,)), dma((4,)),
+                dma((ITERS, n)), dma((ITERS, n)), dma((ITERS, n)), dma((ITERS, n)),
+                dma((ITERS,)), dma((ITERS,)), dma((3,)), dma((3,)),
             ],
             compiler_params=pltpu.CompilerParams(
                 collective_id=0, has_side_effects=True, vmem_limit_bytes=VMEM_BYTES
             ),
             name="exchange_and_sweeps",
-        )(picked, wanted, src, tgt)
+        )(pair_source, pair_target, pair_count, src, tgt)
     pairs = reps * n
     with jax.named_scope("gradient"):
-        grad = pl.pallas_call(
+        grad, source_dual, target_dual = pl.pallas_call(
             functools.partial(gradient_kernel, pairs, blocks, scale),
-            out_shape=shape((blocks, BLOCK, dim), f32),
-            in_specs=[smem, hbm, vmem, vmem, vmem],
-            out_specs=hbm,
+            out_shape=(
+                shape((blocks, BLOCK, dim), f32),
+                shape((blocks, BLOCK), f32),
+                shape((blocks, BLOCK), f32),
+            ),
+            in_specs=[smem, hbm, vmem, vmem, vmem, vmem, vmem],
+            out_specs=(hbm, vmem, vmem),
             scratch_shapes=[
                 pltpu.VMEM((pairs, BLOCK, dim), bf16),
                 pltpu.VMEM((blocks, BLOCK, dim), f32),
@@ -493,6 +493,8 @@
             a_rows.reshape(pairs, BLOCK),
             b_rows,
             tgt,
+            source_dual,
+            target_dual,
         )
     return source_dual.reshape(-1), target_dual.reshape(-1), grad.reshape(rows, dim)
 

time: 83 us -> 76.4 us (0.920)
  Pallas kernels: 78.9 us -> 74.9 us
  other arithmetic: 1.3 us -> 0 us
  local copies, waits for them, and re-layouts: 1.21 us -> 0 us
    pallas_call x1, Pallas kernels: 70.1 us -> 65.5 us  [on_device(): pl.pallas_call(functools.partial(exchange_kernel, n, blocks, half, scale)...]
    unnamed x6 -> x0, local copies, waits for them, and re-layouts: 1.21 us -> none
where the time goes in v3:
time: 76.4 us; the launch traced here: 76.2 us
  Pallas kernels  74.9 us (98%)
  between operations  1.29 us (2%)
    pallas_call x1, Pallas kernels, on_device(): pl.pallas_call(functools.partial(exchange_kernel, n, blocks, half, scale)...  65.5 us
    pallas_call x1, Pallas kernels, on_device(): pl.pallas_call(functools.partial(gradient_kernel, pairs, blocks, scale),...  9.48 us

profile of v3, /device:TPU:0, one launch (start us, length us, event | category | flops | bytes accessed | tf_op | source)
XLA Modules:
  0.0 76.2 jit_solution(2556112244393893290)
XLA Ops:
  1.3 65.5 %exchange_and_sweeps.1 = (bf16[2,16,128,256]{3,2,1,0:T(8,128)(2,1)}, s32[2,16,128]{2,1,0:T(8,128)}, f32[2,16,128]{2,1,0:T(8,128)}, f32[24,128]{1,0:T(8,128)}, f32[24,128]{1,0:T(8,128)}, /*index=5*/f32[24,128]{1,0:T(8,128)}) custom-call(s32[16]{0:T(128)} %pair_source.1, s32[16]{0:T(128)} %pair_target.1, s32[1]{0:T(128)S(6)} %copy.8.pair_count, ...), custom_call_target="tpu_custom_call" | custom-call | tf_op jit(solution)/shard_map/exchange_and_sweeps/exchange_and_sweeps/pallas_call | solution.py:417
  66.7 9.5 %gradient.1 = (f32[24,128,256]{2,1,0:T(8,128)}, f32[24,128]{1,0:T(8,128)}, f32[24,128]{1,0:T(8,128)}) custom-call(s32[32,128]{1,0:T(8,128)} %bitcast.12, bf16[32,128,256]{2,1,0:T(8,128)(2,1)} %bitcast.10, f32[32,128]{1,0:T(8,128)} %bitcast.13, f32[24,128]{1,0:T(8,128)} %get-tuple-element.15.b_rows, bf16[24,128,256]{2,1,0:T(8,128)(2,1)} %bitcast.9, ...), custom_call_target="tpu_custom_call" | custom-call | tf_op jit(solution)/shard_map/gradient/gradient/pallas_call | solution.py:471

commit v4 on v3

--- a/solution.py
+++ b/solution.py
@@ -218,20 +218,25 @@
             def _():
                 x_copy(peer, peer).wait_recv()
 
-        for peer in peers:
-            pick = local_id(peer)
-            grid = lax.dot_general(
+        picks = [local_id(peer) for peer in peers]
+        grids = [
+            lax.dot_general(
                 rx[peer], tgt[pick], (((1,), (1,)), ((), ())), preferred_element_type=jnp.float32
             ) * (2.0 * scale)
-            grid_t = jnp.transpose(grid)
-            score[peer] = grid
-            score_t[peer] = grid_t
-            stats_out[0, peer] = logsum(b_col[pick] + grid_t)
+            for peer, pick in zip(peers, picks)
+        ]
+        turned = [jnp.transpose(grid) for grid in grids]
+        rows = [logsum(b_col[pick] + grid_t) for pick, grid_t in zip(picks, turned)]
+        for peer, row in zip(peers, rows):
+            stats_out[0, peer] = row
         for d, peer in zip(offsets, peers):
             @pl.when(d > 0)
             def _():
                 stat_copy(0, peer, me).start()
 
+        for peer, grid, grid_t in zip(peers, grids, turned):
+            score[peer] = grid
+            score_t[peer] = grid_t
         for peer in peers:
             keep_copy(peer).start()
             forward_copy(peer, side).start()
@@ -251,8 +256,9 @@
 
         grouped(n, 8, stat_row)
         values, keys = stat_rows[...], source_keys[...]
-        for b in range(blocks):
-            rep_out[it, b:b + 1, :] = combine(values, keys, b)
+        rows = [combine(values, keys, b) for b in range(blocks)]
+        for b, row in enumerate(rows):
+            rep_out[it, b:b + 1, :] = row
         swap(it).start()
         swap(it).wait_recv()
         top = jnp.maximum(rep_out[it], rep_in[it])
@@ -260,11 +266,12 @@
         a_src[...] = -(top + jnp.log(total))
 
         def send_a(d):
-            peer = lax.rem(me + d, n)
+            peer = lax.rem(me + n // 2 + d, n)
             a_send[it, peer] = a_src[pl.ds(jnp.maximum(source_pick[peer], 0), 1), :]
             a_copy(it, peer, me).start()
 
-        loop(1, n, send_a)
+        loop(0, n // 2, send_a)
+        loop(n // 2 + 1, n, send_a)
         a_in[it, me] = a_src[pl.ds(jnp.maximum(source_pick[me], 0), 1), :]
 
         def take_a(d):
@@ -283,13 +290,16 @@
 
         def column_visits(chunk):
             base = chunk * 16
-            for k, column in enumerate(columns_of(a_rows[pl.ds(pl.multiple_of(base, 16), 16), :])):
-                stat_rows[pl.ds(base + k, 1), :] = logsum(column + score[base + k])
+            columns = columns_of(a_rows[pl.ds(pl.multiple_of(base, 16), 16), :])
+            rows = [logsum(column + score[base + k]) for k, column in enumerate(columns)]
+            for k, row in enumerate(rows):
+                stat_rows[pl.ds(base + k, 1), :] = row
 
         loop(0, n // 16, column_visits)
         values, keys = stat_rows[...], id_keys[...]
-        for b in range(half):
-            b_pad[b:b + 1, :] = -combine(values, keys, b + first)
+        rows = [-combine(values, keys, b + first) for b in range(half)]
+        for b, row in enumerate(rows):
+            b_pad[b:b + 1, :] = row
         if it + 1 == ITERS:
             b_all[side] = b_pad[0:half, :]
         else:
@@ -297,17 +307,16 @@
                 b_col[first + b] = column
 
             def next_rows(group):
-                for k in range(4):
-                    q = lax.rem(me + group * 4 + k, n)
-                    stats_out[it + 1, q] = logsum(b_col[local_id(q)] + score_t[q])
-                for k in range(4):
-                    d = group * 4 + k
-
-                    @pl.when(d > 0)
+                peers = [lax.rem(me + n // 2 + group * 8 + k, n) for k in range(8)]
+                rows = [logsum(b_col[local_id(q)] + score_t[q]) for q in peers]
+                for q, row in zip(peers, rows):
+                    stats_out[it + 1, q] = row
+                for q in peers:
+                    @pl.when(q != me)
                     def _():
-                        stat_copy(it + 1, lax.rem(me + d, n), me).start()
-
-            loop(0, n // 4, next_rows)
+                        stat_copy(it + 1, q, me).start()
+
+            loop(0, n // 8, next_rows)
 
     tail_copy(2, b_all, side).start()
     source_out[...] = EPSILON * (a_src[...] + x_sq[...])
@@ -341,8 +350,8 @@
 
 
 def gradient_kernel(
-    pairs, blocks, scale, ids, rx_hbm, a_rows, b_rows, tgt, source_in, target_in,
-    out, source_out, target_out, rx, grad, b_col, mass, sems, out_sems,
+    pairs, blocks, scale, ids, rx_hbm, a_rows, b_rows, tgt_hbm, source_in, target_in,
+    out, source_out, target_out, rx, tgt, grad, b_col, mass, sems, out_sems,
 ):
     groups = pairs // 4
 
@@ -353,6 +362,8 @@
     def store(b):
         return pltpu.make_async_copy(grad.at[b], out.at[b], out_sems.at[b])
 
+    load_tgt = pltpu.make_async_copy(tgt_hbm, tgt, out_sems.at[blocks])
+    load_tgt.start()
     loop(0, groups, lambda group: fetch(group).start())
     source_out[...] = source_in[...]
     target_out[...] = target_in[...]
@@ -364,6 +375,7 @@
         mass[b] = jnp.zeros((BLOCK, BLOCK), jnp.float32)
 
     grouped(blocks, 4, prepare)
+    load_tgt.wait()
 
     def visit(group):
         fetch(group).wait()
@@ -475,15 +487,16 @@
                 shape((blocks, BLOCK), f32),
                 shape((blocks, BLOCK), f32),
             ),
-            in_specs=[smem, hbm, vmem, vmem, vmem, vmem, vmem],
+            in_specs=[smem, hbm, vmem, vmem, hbm, vmem, vmem],
             out_specs=(hbm, vmem, vmem),
             scratch_shapes=[
                 pltpu.VMEM((pairs, BLOCK, dim), bf16),
+                pltpu.VMEM((blocks, BLOCK, dim), bf16),
                 pltpu.VMEM((blocks, BLOCK, dim), f32),
                 pltpu.VMEM((blocks, BLOCK, BLOCK), f32),
                 pltpu.VMEM((blocks, BLOCK, BLOCK), f32),
                 dma((pairs // 4,)),
-                dma((blocks,)),
+                dma((blocks + 1,)),
             ],
             compiler_params=pltpu.CompilerParams(vmem_limit_bytes=VMEM_BYTES),
             name="gradient",

time: 76.4 us -> 76.3 us (level)
  no operation moved by 1% of the time
where the time goes in v4:
time: 76.3 us; the launch traced here: 76.1 us
  Pallas kernels  74.8 us (98%)
  between operations  1.29 us (2%)
    pallas_call x1, Pallas kernels, on_device(): pl.pallas_call(functools.partial(exchange_kernel, n, blocks, half, scale)...  65.3 us
    pallas_call x1, Pallas kernels, on_device(): pl.pallas_call(functools.partial(gradient_kernel, pairs, blocks, scale),...  9.5 us

profile of v4, /device:TPU:0, one launch (start us, length us, event | category | flops | bytes accessed | tf_op | source)
XLA Modules:
  0.0 76.1 jit_solution(1959941214457935383)
XLA Ops:
  1.3 65.3 %exchange_and_sweeps.1 = (bf16[2,16,128,256]{3,2,1,0:T(8,128)(2,1)}, s32[2,16,128]{2,1,0:T(8,128)}, f32[2,16,128]{2,1,0:T(8,128)}, f32[24,128]{1,0:T(8,128)}, f32[24,128]{1,0:T(8,128)}, /*index=5*/f32[24,128]{1,0:T(8,128)}) custom-call(s32[16]{0:T(128)} %pair_source.1, s32[16]{0:T(128)} %pair_target.1, s32[1]{0:T(128)S(6)} %copy.8.pair_count, ...), custom_call_target="tpu_custom_call" | custom-call | tf_op jit(solution)/shard_map/exchange_and_sweeps/exchange_and_sweeps/pallas_call | solution.py:429
  66.6 9.5 %gradient.1 = (f32[24,128,256]{2,1,0:T(8,128)}, f32[24,128]{1,0:T(8,128)}, f32[24,128]{1,0:T(8,128)}) custom-call(s32[32,128]{1,0:T(8,128)} %bitcast.12, bf16[32,128,256]{2,1,0:T(8,128)(2,1)} %bitcast.10, f32[32,128]{1,0:T(8,128)} %bitcast.13, f32[24,128]{1,0:T(8,128)} %get-tuple-element.15.b_rows, bf16[24,128,256]{2,1,0:T(8,128)(2,1)} %bitcast.9, ...), custom_call_target="tpu_custom_call" | custom-call | tf_op jit(solution)/shard_map/gradient/gradient/pallas_call | solution.py:483

commit v5 on v4

--- a/solution.py
+++ b/solution.py
@@ -21,6 +21,21 @@
         return carry
 
     lax.fori_loop(lower, upper, step, 0)
+
+
+def spread(lower, upper, body):
+    if upper - lower <= 16:
+        for i in range(lower, upper):
+            body(i)
+    else:
+        loop(lower, upper, body)
+
+
+def unless_zero(d, action):
+    if not isinstance(d, int):
+        pl.when(d > 0)(action)
+    elif d:
+        action()
 
 
 def grouped(total, size, body):
@@ -66,7 +81,15 @@
 
 
 def in_turn(t, n):
+    if isinstance(t, int):
+        return (t + 1) // 2 % (n // 2) if t % 2 else n // 2 + t // 2
     return jnp.where(t % 2 == 0, n // 2 + t // 2, lax.rem((t + 1) // 2, n // 2))
+
+
+def far_first(t, n):
+    if isinstance(t, int):
+        return (n // 2 + t) if t < n // 2 else (t - n // 2 + 1) % (n // 2)
+    return jnp.where(t < n // 2, n // 2 + t, lax.rem(t - n // 2 + 1, n // 2))
 
 
 def exchange_kernel(
@@ -143,15 +166,25 @@
     def stat_copy(it, peer, slot):
         return to_peer(
             stats_out.at[it, peer], stats_in.at[it, slot],
-            stat_send.at[it, peer], stat_recv.at[it, slot], peer,
-        )
+            stat_send.at[it], stat_recv.at[it], peer,
+        )
+
+    def stat_total(it):
+        part = pl.ds(0, n - 1)
+        return to_twin(
+            stats_out.at[it, part], stats_in.at[it, part], stat_send.at[it], stat_recv.at[it]
+        )
+
+    def a_total(it):
+        part = pl.ds(0, n - 1)
+        return to_twin(a_send.at[it, part], a_in.at[it, part], a_ssem.at[it], a_rsem.at[it])
 
     def swap(it):
         return to_twin(rep_out.at[it], rep_in.at[it], rep_send.at[it], rep_recv.at[it])
 
     def a_copy(it, peer, slot):
         return to_peer(
-            a_send.at[it, peer], a_in.at[it, slot], a_ssem.at[it, peer], a_rsem.at[it, slot], peer
+            a_send.at[it, peer], a_in.at[it, slot], a_ssem.at[it], a_rsem.at[it], peer
         )
 
     def keep_copy(slot):
@@ -173,7 +206,7 @@
         out_x[peer] = src[jnp.maximum(source_pick[peer], 0)]
         x_copy(peer, me).start()
 
-    loop(0, n - 1, lambda t: send_block(in_turn(t, n)))
+    spread(0, n - 1, lambda t: send_block(in_turn(t, n)))
     rx[me] = src[jnp.maximum(source_pick[me], 0)]
     ids_in[me] = want_rows[me]
     load_tgt.wait()
@@ -214,9 +247,7 @@
         offsets = [in_turn(group * 4 + k, n) for k in range(4)]
         peers = [flipped(me, d, n) for d in offsets]
         for d, peer in zip(offsets, peers):
-            @pl.when(d > 0)
-            def _():
-                x_copy(peer, peer).wait_recv()
+            unless_zero(d, lambda peer=peer: x_copy(peer, peer).wait_recv())
 
         picks = [local_id(peer) for peer in peers]
         grids = [
@@ -230,9 +261,7 @@
         for peer, row in zip(peers, rows):
             stats_out[0, peer] = row
         for d, peer in zip(offsets, peers):
-            @pl.when(d > 0)
-            def _():
-                stat_copy(0, peer, me).start()
+            unless_zero(d, lambda peer=peer: stat_copy(0, peer, me).start())
 
         for peer, grid, grid_t in zip(peers, grids, turned):
             score[peer] = grid
@@ -241,14 +270,28 @@
             keep_copy(peer).start()
             forward_copy(peer, side).start()
 
-    loop(0, n // 4, arrivals)
+    spread(0, n // 4, arrivals)
+
+    def finish_blocks(d):
+        peer = lax.rem(me + d, n)
+        id_copy(peer, me).wait_send()
+        x_copy(peer, me).wait_send()
+
+    def finish_forwards(q):
+        keep_copy(q).wait()
+        forward_copy(q, other).wait_recv()
+        forward_copy(q, side).wait_send()
 
     for it in range(ITERS):
-        def take_stats(d):
-            peer = lax.rem(me + d, n)
-            stat_copy(it, peer, peer).wait_recv()
-
-        loop(1, n, take_stats)
+        if it == 1:
+            loop(1, n, finish_blocks)
+        if it == 2:
+            loop(0, n, finish_forwards)
+        if it > 0:
+            stat_total(it - 1).wait_send()
+            a_total(it - 1).wait_send()
+            swap(it - 1).wait_send()
+        stat_total(it).wait_recv()
         stats_in[it, me] = stats_out[it, me]
 
         def stat_row(p):
@@ -266,19 +309,14 @@
         a_src[...] = -(top + jnp.log(total))
 
         def send_a(d):
-            peer = lax.rem(me + n // 2 + d, n)
+            peer = lax.rem(me + far_first(d, n), n)
             a_send[it, peer] = a_src[pl.ds(jnp.maximum(source_pick[peer], 0), 1), :]
             a_copy(it, peer, me).start()
 
-        loop(0, n // 2, send_a)
-        loop(n // 2 + 1, n, send_a)
+        spread(0, n - 1, send_a)
         a_in[it, me] = a_src[pl.ds(jnp.maximum(source_pick[me], 0), 1), :]
 
-        def take_a(d):
-            peer = lax.rem(me + d, n)
-            a_copy(it, peer, peer).wait_recv()
-
-        loop(1, n, take_a)
+        a_total(it).wait_recv()
 
         def a_row(q):
             a_rows[pl.ds(q, 1), :] = a_in[it, q]
@@ -307,38 +345,22 @@
                 b_col[first + b] = column
 
             def next_rows(group):
-                peers = [lax.rem(me + n // 2 + group * 8 + k, n) for k in range(8)]
+                offsets = [far_first(group * 8 + k, n) for k in range(8)]
+                peers = [lax.rem(me + d, n) for d in offsets]
                 rows = [logsum(b_col[local_id(q)] + score_t[q]) for q in peers]
                 for q, row in zip(peers, rows):
                     stats_out[it + 1, q] = row
-                for q in peers:
-                    @pl.when(q != me)
-                    def _():
-                        stat_copy(it + 1, q, me).start()
-
-            loop(0, n // 8, next_rows)
+                for d, q in zip(offsets, peers):
+                    unless_zero(d, lambda q=q: stat_copy(it + 1, q, me).start())
+
+            spread(0, n // 8, next_rows)
 
     tail_copy(2, b_all, side).start()
     source_out[...] = EPSILON * (a_src[...] + x_sq[...])
 
-    def finish_local(q):
-        keep_copy(q).wait()
-        forward_copy(q, other).wait_recv()
-        forward_copy(q, side).wait_send()
-
-    loop(0, n, finish_local)
-
-    def finish_sends(d):
-        peer = lax.rem(me + d, n)
-        id_copy(peer, me).wait_send()
-        x_copy(peer, me).wait_send()
-        for it in range(ITERS):
-            stat_copy(it, peer, me).wait_send()
-            a_copy(it, peer, me).wait_send()
-
-    loop(1, n, finish_sends)
-    for it in range(ITERS):
-        swap(it).wait_send()
+    stat_total(ITERS - 1).wait_send()
+    a_total(ITERS - 1).wait_send()
+    swap(ITERS - 1).wait_send()
     for k, ref in enumerate((ids_all, a_all, b_all)):
         tail_copy(k, ref, other).wait_recv()
         tail_copy(k, ref, side).wait_send()
@@ -470,7 +492,7 @@
                 pltpu.VMEM((blocks, BLOCK), f32),
                 dma((3,)),
                 dma((n,)), dma((n,)), dma((n,)), dma((n,)), dma((n,)), dma((n,)), dma((n,)),
-                dma((ITERS, n)), dma((ITERS, n)), dma((ITERS, n)), dma((ITERS, n)),
+                dma((ITERS,)), dma((ITERS,)), dma((ITERS,)), dma((ITERS,)),
                 dma((ITERS,)), dma((ITERS,)), dma((3,)), dma((3,)),
             ],
             compiler_params=pltpu.CompilerParams(

time: 76.3 us -> 74.3 us (0.974)
  Pallas kernels: 74.8 us -> 72.8 us
    pallas_call x1, Pallas kernels: 65.3 us -> 63.3 us  [on_device(): pl.pallas_call(functools.partial(exchange_kernel, n, blocks, half, scale)...]
where the time goes in v5:
time: 74.3 us; the launch traced here: 74.1 us
  Pallas kernels  72.8 us (98%)
  between operations  1.29 us (2%)
    pallas_call x1, Pallas kernels, on_device(): pl.pallas_call(functools.partial(exchange_kernel, n, blocks, half, scale)...  63.3 us
    pallas_call x1, Pallas kernels, on_device(): pl.pallas_call(functools.partial(gradient_kernel, pairs, blocks, scale),...  9.5 us

profile of v5, /device:TPU:0, one launch (start us, length us, event | category | flops | bytes accessed | tf_op | source)
XLA Modules:
  0.0 74.1 jit_solution(5451353441352265112)
XLA Ops:
  1.3 63.3 %exchange_and_sweeps.1 = (bf16[2,16,128,256]{3,2,1,0:T(8,128)(2,1)}, s32[2,16,128]{2,1,0:T(8,128)}, f32[2,16,128]{2,1,0:T(8,128)}, f32[24,128]{1,0:T(8,128)}, f32[24,128]{1,0:T(8,128)}, /*index=5*/f32[24,128]{1,0:T(8,128)}) custom-call(s32[16]{0:T(128)} %pair_source.1, s32[16]{0:T(128)} %pair_target.1, s32[1]{0:T(128)S(6)} %copy.8.pair_count, ...), custom_call_target="tpu_custom_call" | custom-call | tf_op jit(solution)/shard_map/exchange_and_sweeps/exchange_and_sweeps/pallas_call | solution.py:451
  64.6 9.5 %gradient.1 = (f32[24,128,256]{2,1,0:T(8,128)}, f32[24,128]{1,0:T(8,128)}, f32[24,128]{1,0:T(8,128)}) custom-call(s32[32,128]{1,0:T(8,128)} %bitcast.12, bf16[32,128,256]{2,1,0:T(8,128)(2,1)} %bitcast.10, f32[32,128]{1,0:T(8,128)} %bitcast.13, f32[24,128]{1,0:T(8,128)} %get-tuple-element.15.b_rows, bf16[24,128,256]{2,1,0:T(8,128)(2,1)} %bitcast.9, ...), custom_call_target="tpu_custom_call" | custom-call | tf_op jit(solution)/shard_map/gradient/gradient/pallas_call | solution.py:505

commit v6 on v5

--- a/solution.py
+++ b/solution.py
@@ -56,10 +56,6 @@
     return out
 
 
-def as_column(row):
-    return jnp.transpose(jnp.broadcast_to(row, (BLOCK, BLOCK)))
-
-
 def columns_of(rows):
     turned = jnp.transpose(rows)
     return [jnp.broadcast_to(turned[:, k:k + 1], (BLOCK, BLOCK)) for k in range(rows.shape[0])]
@@ -67,8 +63,14 @@
 
 def square_row(block):
     values = block.astype(jnp.float32)
-    column = jnp.sum(values * values, axis=1, keepdims=True)
-    return jnp.transpose(jnp.broadcast_to(column, (BLOCK, BLOCK)))[0:1, :]
+    squares = values * values
+    high = squares.astype(jnp.bfloat16)
+    low = (squares - high.astype(jnp.float32)).astype(jnp.bfloat16)
+    ones = jnp.ones((8, block.shape[1]), jnp.bfloat16)
+    along = (((1,), (1,)), ((), ()))
+    total = lax.dot_general(ones, high, along, preferred_element_type=jnp.float32)
+    total += lax.dot_general(ones, low, along, preferred_element_type=jnp.float32)
+    return total[0:1, :]
 
 
 def logsum(terms):
@@ -216,12 +218,12 @@
         x_sq[pl.ds(b, 1), :] = scale * square_row(src[b])
 
     def target_squares(b):
-        row = scale * square_row(tgt[b])
-        y_sq[pl.ds(b, 1), :] = row
-        b_col[b] = as_column(-row)
-
-    loop(0, blocks, source_squares)
-    loop(0, blocks, target_squares)
+        y_sq[pl.ds(b, 1), :] = scale * square_row(tgt[b])
+
+    grouped(blocks, 4, target_squares)
+    grouped(blocks, 4, source_squares)
+    for b, column in enumerate(columns_of(y_sq[...])):
+        b_col[b] = -column
 
     def take_id(d):
         peer = lax.rem(me + d, n)
@@ -375,10 +377,10 @@
     pairs, blocks, scale, ids, rx_hbm, a_rows, b_rows, tgt_hbm, source_in, target_in,
     out, source_out, target_out, rx, tgt, grad, b_col, mass, sems, out_sems,
 ):
-    groups = pairs // 4
+    groups = pairs // 8
 
     def fetch(group):
-        part = pl.ds(group * 4, 4)
+        part = pl.ds(group * 8, 8)
         return pltpu.make_async_copy(rx_hbm.at[part], rx.at[part], sems.at[group])
 
     def store(b):
@@ -402,8 +404,8 @@
     def visit(group):
         fetch(group).wait()
         results = []
-        for k in range(4):
-            q = group * 4 + k
+        for k in range(8):
+            q = group * 8 + k
             target = ids[q, 0]
             pick = jnp.maximum(target, 0)
             grid = lax.dot_general(
@@ -517,7 +519,7 @@
                 pltpu.VMEM((blocks, BLOCK, dim), f32),
                 pltpu.VMEM((blocks, BLOCK, BLOCK), f32),
                 pltpu.VMEM((blocks, BLOCK, BLOCK), f32),
-                dma((pairs // 4,)),
+                dma((pairs // 8,)),
                 dma((blocks + 1,)),
             ],
             compiler_params=pltpu.CompilerParams(vmem_limit_bytes=VMEM_BYTES),

time: 74.3 us -> 72.7 us (0.978)
  Pallas kernels: 72.8 us -> 71.2 us
    pallas_call x1, Pallas kernels: 9.5 us -> 7.93 us  [on_device(): pl.pallas_call(functools.partial(gradient_kernel, pairs, blocks, scale),...]
where the time goes in v6:
time: 72.7 us; the launch traced here: 72.5 us
  Pallas kernels  71.2 us (98%)
  between operations  1.29 us (2%)
    pallas_call x1, Pallas kernels, on_device(): pl.pallas_call(functools.partial(exchange_kernel, n, blocks, half, scale)...  63.3 us
    pallas_call x1, Pallas kernels, on_device(): pl.pallas_call(functools.partial(gradient_kernel, pairs, blocks, scale),...  7.93 us

profile of v6, /device:TPU:0, one launch (start us, length us, event | category | flops | bytes accessed | tf_op | source)
XLA Modules:
  0.0 72.5 jit_solution(9157380996370765187)
XLA Ops:
  1.3 63.3 %exchange_and_sweeps.1 = (bf16[2,16,128,256]{3,2,1,0:T(8,128)(2,1)}, s32[2,16,128]{2,1,0:T(8,128)}, f32[2,16,128]{2,1,0:T(8,128)}, f32[24,128]{1,0:T(8,128)}, f32[24,128]{1,0:T(8,128)}, /*index=5*/f32[24,128]{1,0:T(8,128)}) custom-call(s32[16]{0:T(128)} %pair_source.1, s32[16]{0:T(128)} %pair_target.1, s32[1]{0:T(128)S(6)} %copy.8.pair_count, ...), custom_call_target="tpu_custom_call" | custom-call | tf_op jit(solution)/shard_map/exchange_and_sweeps/exchange_and_sweeps/pallas_call | solution.py:453
  64.6 7.9 %gradient.1 = (f32[24,128,256]{2,1,0:T(8,128)}, f32[24,128]{1,0:T(8,128)}, f32[24,128]{1,0:T(8,128)}) custom-call(s32[32,128]{1,0:T(8,128)} %bitcast.12, bf16[32,128,256]{2,1,0:T(8,128)(2,1)} %bitcast.10, f32[32,128]{1,0:T(8,128)} %bitcast.13, f32[24,128]{1,0:T(8,128)} %get-tuple-element.15.b_rows, bf16[24,128,256]{2,1,0:T(8,128)(2,1)} %bitcast.9, ...), custom_call_target="tpu_custom_call" | custom-call | tf_op jit(solution)/shard_map/gradient/gradient/pallas_call | solution.py:507

commit v7 on v6

--- a/solution.py
+++ b/solution.py
@@ -377,10 +377,10 @@
     pairs, blocks, scale, ids, rx_hbm, a_rows, b_rows, tgt_hbm, source_in, target_in,
     out, source_out, target_out, rx, tgt, grad, b_col, mass, sems, out_sems,
 ):
-    groups = pairs // 8
+    groups = pairs // 16
 
     def fetch(group):
-        part = pl.ds(group * 8, 8)
+        part = pl.ds(group * 16, 16)
         return pltpu.make_async_copy(rx_hbm.at[part], rx.at[part], sems.at[group])
 
     def store(b):
@@ -404,8 +404,8 @@
     def visit(group):
         fetch(group).wait()
         results = []
-        for k in range(8):
-            q = group * 8 + k
+        for k in range(16):
+            q = group * 16 + k
             target = ids[q, 0]
             pick = jnp.maximum(target, 0)
             grid = lax.dot_general(
@@ -519,7 +519,7 @@
                 pltpu.VMEM((blocks, BLOCK, dim), f32),
                 pltpu.VMEM((blocks, BLOCK, BLOCK), f32),
                 pltpu.VMEM((blocks, BLOCK, BLOCK), f32),
-                dma((pairs // 8,)),
+                dma((pairs // 16,)),
                 dma((blocks + 1,)),
             ],
             compiler_params=pltpu.CompilerParams(vmem_limit_bytes=VMEM_BYTES),

time: 72.7 us -> 72.1 us (level)
  no operation moved by 1% of the time
where the time goes in v7:
time: 72.1 us; the launch traced here: 71.9 us
  Pallas kernels  70.6 us (98%)
  between operations  1.29 us (2%)
    pallas_call x1, Pallas kernels, on_device(): pl.pallas_call(functools.partial(exchange_kernel, n, blocks, half, scale)...  63.3 us
    pallas_call x1, Pallas kernels, on_device(): pl.pallas_call(functools.partial(gradient_kernel, pairs, blocks, scale),...  7.3 us

profile of v7, /device:TPU:0, one launch (start us, length us, event | category | flops | bytes accessed | tf_op | source)
XLA Modules:
  0.0 71.9 jit_solution(17716406421416471895)
XLA Ops:
  1.3 63.3 %exchange_and_sweeps.1 = (bf16[2,16,128,256]{3,2,1,0:T(8,128)(2,1)}, s32[2,16,128]{2,1,0:T(8,128)}, f32[2,16,128]{2,1,0:T(8,128)}, f32[24,128]{1,0:T(8,128)}, f32[24,128]{1,0:T(8,128)}, /*index=5*/f32[24,128]{1,0:T(8,128)}) custom-call(s32[16]{0:T(128)} %pair_source.1, s32[16]{0:T(128)} %pair_target.1, s32[1]{0:T(128)S(6)} %copy.8.pair_count, ...), custom_call_target="tpu_custom_call" | custom-call | tf_op jit(solution)/shard_map/exchange_and_sweeps/exchange_and_sweeps/pallas_call | solution.py:453
  64.6 7.3 %gradient.1 = (f32[24,128,256]{2,1,0:T(8,128)}, f32[24,128]{1,0:T(8,128)}, f32[24,128]{1,0:T(8,128)}) custom-call(s32[32,128]{1,0:T(8,128)} %bitcast.12, bf16[32,128,256]{2,1,0:T(8,128)(2,1)} %bitcast.10, f32[32,128]{1,0:T(8,128)} %bitcast.13, f32[24,128]{1,0:T(8,128)} %get-tuple-element.15.b_rows, bf16[24,128,256]{2,1,0:T(8,128)(2,1)} %bitcast.9, ...), custom_call_target="tpu_custom_call" | custom-call | tf_op jit(solution)/shard_map/gradient/gradient/pallas_call | solution.py:507
